TPU v7x, 1024 devices: a whole 4x8x16 slice. The times are simulated.
1024 devices in a mesh: expert: 32 (over z_hi, x, core), dp: 32 (over z_lo, y).
Axes of the slice: x: 4, y: 8, z: 16 (z_hi: 4, z_lo: 4; z = z_hi * 4 + z_lo), core: 2. Of those that a mesh axis runs over, the one named last changes fastest.
Arguments:
- tokens: bfloat16 [256, 256, 640], P('dp', None, 'expert'), may hold values from -40 to 40
- slot_params: bfloat16 [640, 128], P('expert'), may hold values from -40 to 40
- w_in: bfloat16 [128, 640, 5120], P('expert', None, 'dp'), may hold values from -0.25 to 0.25
- w_out: bfloat16 [128, 5120, 640], P('expert', 'dp'), may hold values from -0.078125 to 0.078125
- out_grad: bfloat16 [256, 256, 640], P('dp', None, 'expert'), may hold values from -6 to 6
Outputs:
- grad_tokens: bfloat16 [256, 256, 640], P('dp', None, 'expert')
- grad_w_in: bfloat16 [128, 640, 5120], P('expert', None, 'dp')
- grad_w_out: bfloat16 [128, 5120, 640], P('expert', 'dp')
All inputs are finite; a program needn't handle non-finite values.
Results may differ from a plain program's by a relative error of at most 0.034.
Values may be sent and summed in bfloat16 or wider, within the bound.
A program may use at most 32 MiB of HBM per device.

v0:
```python
import jax
import jax.numpy as jnp
from jax import lax
from jax.sharding import PartitionSpec as P

SCALE = 32.0
EPS = 1e-06


def local(tokens, slot_params, w_in, w_out, out_grad):
    xfull = tokens.astype(jnp.float32)
    pfull = slot_params.astype(jnp.float32)
    prod = jnp.einsum("imd,ds->ims", tokens, slot_params, preferred_element_type=jnp.float32)
    row_sq = jnp.sum(xfull * xfull, -1)
    col_sq = jnp.sum(pfull * pfull, 0)
    prod, row_sq, col_sq = lax.psum((prod, row_sq, col_sq), "expert")
    row_inv = lax.rsqrt(row_sq + EPS)
    col_inv = lax.rsqrt(col_sq + EPS)
    logits = SCALE * prod * row_inv[:, :, None] * col_inv[None, None, :]
    expo = jnp.exp(logits)
    dispatch = expo / jnp.sum(expo, 1, keepdims=True)
    combine = expo / jnp.sum(expo, 2, keepdims=True)
    dispatch_b = dispatch.astype(jnp.bfloat16)
    combine_b = combine.astype(jnp.bfloat16)
    slot_in = jnp.einsum(
        "ims,imd->isd", dispatch_b, tokens, preferred_element_type=jnp.float32
    ).astype(jnp.bfloat16)
    slot_grad = jnp.einsum(
        "ims,imd->isd", combine_b, out_grad, preferred_element_type=jnp.float32
    ).astype(jnp.bfloat16)
    rows, grads = (
        lax.all_to_all(slot_in, "expert", split_axis=1, concat_axis=2, tiled=True),
        lax.all_to_all(slot_grad, "expert", split_axis=1, concat_axis=2, tiled=True),
    )
    rows, grads = (
        lax.all_gather(rows, "dp", axis=0, tiled=True),
        lax.all_gather(grads, "dp", axis=0, tiled=True),
    )
    hidden = jnp.einsum("ied,edf->ief", rows, w_in, preferred_element_type=jnp.float32)
    act_b = jax.nn.gelu(hidden).astype(jnp.bfloat16)
    out_part = jnp.einsum("ief,efd->ied", act_b, w_out, preferred_element_type=jnp.float32)
    dact = jnp.einsum("ied,efd->ief", grads, w_out, preferred_element_type=jnp.float32)
    _, pull = jax.vjp(jax.nn.gelu, hidden)
    dhid = pull(dact)[0].astype(jnp.bfloat16)
    grad_w_out = jnp.einsum(
        "ief,ied->efd", act_b, grads, preferred_element_type=jnp.float32
    ).astype(jnp.bfloat16)
    grad_w_in = jnp.einsum("ied,ief->edf", rows, dhid, preferred_element_type=jnp.float32).astype(
        jnp.bfloat16
    )
    back_part = jnp.einsum("ief,edf->ied", dhid, w_in, preferred_element_type=jnp.float32)
    summed_out, summed_back = (
        lax.psum_scatter(
            out_part.astype(jnp.bfloat16), "dp", scatter_dimension=0, tiled=True
        ).astype(jnp.float32),
        lax.psum_scatter(
            back_part.astype(jnp.bfloat16), "dp", scatter_dimension=0, tiled=True
        ).astype(jnp.float32),
    )
    slot_out, slot_back = (
        lax.all_to_all(
            summed_out.astype(jnp.bfloat16), "expert", split_axis=2, concat_axis=1, tiled=True
        ),
        lax.all_to_all(
            summed_back.astype(jnp.bfloat16), "expert", split_axis=2, concat_axis=1, tiled=True
        ),
    )
    dcomb = jnp.einsum("imd,isd->ims", out_grad, slot_out, preferred_element_type=jnp.float32)
    ddisp = jnp.einsum("imd,isd->ims", tokens, slot_back, preferred_element_type=jnp.float32)
    dcomb, ddisp = lax.psum((dcomb, ddisp), "expert")
    dlog = combine * (dcomb - jnp.sum(combine * dcomb, 2, keepdims=True))
    dlog = dlog + dispatch * (ddisp - jnp.sum(dispatch * ddisp, 1, keepdims=True))
    centre = jnp.sum(dlog * logits, 2)
    pulled = (SCALE * dlog * col_inv[None, None, :]).astype(jnp.bfloat16)
    backward = jnp.einsum("ims,ds->imd", pulled, slot_params, preferred_element_type=jnp.float32)
    direct = jnp.einsum("ims,isd->imd", dispatch_b, slot_back, preferred_element_type=jnp.float32)
    grad_tokens = direct + row_inv[:, :, None] * (backward - xfull * (row_inv * centre)[:, :, None])
    return (grad_tokens.astype(jnp.bfloat16), grad_w_in, grad_w_out)


def solution(mesh):
    return jax.shard_map(
        local,
        mesh=mesh,
        in_specs=(
            P("dp", None, "expert"),
            P("expert", None),
            P("expert", None, "dp"),
            P("expert", "dp", None),
            P("dp", None, "expert"),
        ),
        out_specs=(P("dp", None, "expert"), P("expert", None, "dp"), P("expert", "dp", None)),
        check_vma=False,
    )
```

profile of v0, /device:TPU:1, one launch (start us, length us, event | category | flops | bytes accessed | tf_op | source)
XLA Modules:
  0.0 1459.5 jit_solution(2136496479187964865)
XLA Ops:
  7.2 0.0 copy-start
  7.2 0.0 all-reduce.5.cloned.1.call-start
  7.2 2.3 fusion.35
  9.5 0.0 all-reduce.5.cloned.1.call-update
  9.6 0.0 all-gather.5.cloned.1.call-start
  9.7 99.7 %all-reduce = (f32[128]{0:T(128)S(1)}, f32[8,256]{1,0:T(8,128)S(1)}) all-reduce(f32[128]{0:T(128)S(1)} %multiply_reduce_fusion.3, f32[8,256]{1,0:T(8,128)S(1)} %fusion.30), channel_id=1, replica_groups=mesh['expert'=32,'dp'=32] {'expert'}, use_global_device_ids=true, to_apply=%region_4.0 | all-reduce | flops 2176 | bytes 17408 | tf_op jit(solution)/shard_map/psum | solution.py:16
  109.5 269.5 %all-reduce.5.cloned.1.call-done = f32[8,256,128]{2,1,0:T(8,128)} async-done(((f32[8,256,128]{2,1,0:T(8,128)}), f32[8,256,128]{2,1,0:T(8,128)}) %all-reduce.5.cloned.1.call-update) | async-done | bytes 1048592 | tf_op jit(solution)/shard_map/psum | solution.py:16
  379.0 1.9 fusion.24
  380.9 1.7 convolution_convert_fusion.4
  382.6 0.2 copy.45
  382.8 0.3 reshape.18
  383.2 28.2 %all_to_all.72 = bf16[32,2,320]{2,1,0:T(2,128)(2,1)S(1)} all-to-all(bf16[32,2,320]{2,1,0:T(2,128)(2,1)S(1)} %reshape.18), channel_id=1, replica_groups=mesh['expert'=32,'dp'=32] {'expert'}, dimensions={0} | all-to-all | bytes 81920 | tf_op jit(solution)/shard_map/all_to_all | solution.py:32
  411.4 0.4 reshape.19
  411.8 0.1 copy.46
  411.9 1.0 all_to_all.59
  412.8 0.0 all-gather.5.cloned.1.call-update
  412.9 0.0 all-gather.3.cloned.1.call-start
  412.9 0.9 convolution_convert_fusion.5
  413.9 0.2 copy.42
  414.1 0.3 reshape.20
  414.5 18.3 %all_to_all.73 = bf16[32,2,320]{2,1,0:T(2,128)(2,1)S(1)} all-to-all(bf16[32,2,320]{2,1,0:T(2,128)(2,1)S(1)} %reshape.20), channel_id=1, replica_groups=mesh['expert'=32,'dp'=32] {'expert'}, dimensions={0} | all-to-all | bytes 81920 | tf_op jit(solution)/shard_map/all_to_all | solution.py:33
  432.7 0.4 reshape.21
  433.1 0.1 copy.43
  433.2 1.0 all_to_all.55
  434.2 0.0 all-gather.3.cloned.1.call-update
  434.2 0.0 reduce-scatter.9.cloned.1.call-start
  434.2 107.5 %all-gather.5.cloned.1.call-done = bf16[256,4,640]{2,0,1:T(8,128)(2,1)} async-done(((bf16[8,4,640]{2,0,1:T(8,128)(2,1)}), bf16[256,4,640]{2,0,1:T(8,128)(2,1)}) %all-gather.5.cloned.1.call-update) | async-done | bytes 1310736 | tf_op jit(solution)/shard_map/all_gather | solution.py:36
  541.7 1.9 convolution_bitcast_fusion.2
  543.6 0.6 fusion.3
  544.3 1.2 copy.72
  545.5 0.0 reduce-scatter.9.cloned.1.call-update
  545.5 0.0 reduce-scatter.7.cloned.1.call-start
  545.5 153.3 %all-gather.3.cloned.1.call-done = bf16[256,4,640]{2,0,1:T(8,128)(2,1)} async-done(((bf16[8,4,640]{2,0,1:T(8,128)(2,1)}), bf16[256,4,640]{2,0,1:T(8,128)(2,1)}) %all-gather.3.cloned.1.call-update) | async-done | bytes 1310736 | tf_op jit(solution)/shard_map/all_gather | solution.py:37
  698.8 2.1 fusion.21
  700.9 0.6 fusion.2
  701.6 1.2 copy.71
  702.8 0.0 reduce-scatter.7.cloned.1.call-update
  702.8 160.0 %reduce-scatter.9.cloned.1.call-done = bf16[8,2560]{1,0:T(8,128)(2,1)} async-done(((bf16[256,2560]{1,0:T(8,128)(2,1)}), bf16[8,2560]{1,0:T(8,128)(2,1)}) %reduce-scatter.9.cloned.1.call-update) | async-done | bytes 40976
  862.7 1.1 copy.51
  863.9 1.3 reshape.24
  865.2 37.4 %all-to-all-start.3 = ((bf16[32,2,320]{2,1,0:T(2,128)(2,1)}), bf16[32,2,320]{2,1,0:T(2,128)(2,1)S(1)}, u32[]{:S(2)}, u32[]{:S(2)}) async-start(bf16[32,2,320]{2,1,0:T(2,128)(2,1)} %reshape.24), calls=%async_computation.3 | async-start | bytes 98304 | tf_op jit(solution)/shard_map/all_to_all | solution.py:61
  902.6 125.7 %reduce-scatter.7.cloned.1.call-done = bf16[8,2560]{1,0:T(8,128)(2,1)} async-done(((bf16[256,2560]{1,0:T(8,128)(2,1)}), bf16[8,2560]{1,0:T(8,128)(2,1)}) %reduce-scatter.7.cloned.1.call-update) | async-done | bytes 40976
  1028.3 1.1 copy.47
  1029.4 1.3 reshape.22
  1030.8 37.1 %all-to-all-start.2 = ((bf16[32,2,320]{2,1,0:T(2,128)(2,1)}), bf16[32,2,320]{2,1,0:T(2,128)(2,1)S(1)}, u32[]{:S(2)}, u32[]{:S(2)}) async-start(bf16[32,2,320]{2,1,0:T(2,128)(2,1)} %reshape.22), calls=%async_computation.2 | async-start | bytes 98304 | tf_op jit(solution)/shard_map/all_to_all | solution.py:64
  1067.8 0.2 all-reduce.7.cloned.1.call-start
  1068.0 0.5 reshape.25
  1068.5 0.8 copy.66
  1069.4 1.3 convolution_bitcast_fusion.1
  1070.7 11.7 all-to-all-done.2
  1082.4 0.5 reshape.23
  1082.8 0.8 copy.64
  1083.7 0.2 copy.50
  1083.9 1.3 convolution_bitcast_fusion
  1085.3 0.0 all-reduce.7.cloned.1.call-update
  1085.3 1.3 copy-done.1
  1086.6 1.3 convolution_convert_fusion.2
  1087.9 1.4 convolution_convert_fusion.3
  1089.3 0.5 fusion.27
  1089.7 347.4 %all-reduce.7.cloned.1.call-done = (f32[8,256,128]{2,1,0:T(8,128)}, f32[8,256,128]{2,1,0:T(8,128)}) async-done(((f32[8,256,128]{2,1,0:T(8,128)}, f32[8,256,128]{2,1,0:T(8,128)}), (f32[8,256,128]{2,1,0:T(8,128)}, f32[8,256,128]{2,1,0:T(8,128)})) %all-reduce.7.cloned.1.call-update) | async-done | bytes 2097168 | tf_op jit(solution)/shard_map/psum | solution.py:70
  1437.1 2.3 fusion.8
  1439.4 12.2 multiply_reduce_fusion
  1451.6 0.4 fusion.11
  1452.0 0.7 copy.60
  (24 shorter events, 0.1 us)
Async XLA Ops:
  7.2 536.4 %copy-start = (bf16[4,160,640]{2,1,0:T(8,128)(2,1)S(1)}, bf16[4,160,640]{2,1,0:T(8,128)(2,1)}, u32[]{:S(2)}) copy-start(bf16[4,160,640]{2,1,0:T(8,128)(2,1)} %param.8) | copy-start | bytes 2457604
  7.2 2.5 copy-start.3
  7.2 2.4 copy-start.7
  7.2 371.8 %all-reduce.5.cloned.1.call-start = ((), (), s32[]{:S(2)}) async-start(), calls=%async_computation.6 | async-start | bytes 2097152 | tf_op jit(solution)/shard_map/psum | solution.py:16
  9.6 532.1 %all-gather.5.cloned.1.call-start = ((), (), s32[]{:S(2)}) async-start(), calls=%async_computation.8 | async-start | bytes 1351680 | tf_op jit(solution)/shard_map/all_gather | solution.py:36
  382.6 30.3 %copy-start.4 = (f32[8,256,128]{2,1,0:T(8,128)S(1)}, f32[8,256,128]{2,1,0:T(8,128)}, u32[]{:S(2)}) copy-start(f32[8,256,128]{2,1,0:T(8,128)} %all-reduce.5.cloned.1.call-done) | copy-start | bytes 3145732
  382.6 30.3 %copy-start.6 = (bf16[8,256,20]{1,0,2:T(8,128)(2,1)S(1)}, bf16[8,256,20]{1,0,2:T(8,128)(2,1)}, u32[]{:S(2)}) copy-start(bf16[8,256,20]{1,0,2:T(8,128)(2,1)} %param.9) | copy-start | bytes 245764
  412.9 286.0 %all-gather.3.cloned.1.call-start = ((), (), s32[]{:S(2)}) async-start(), calls=%async_computation.7 | async-start | bytes 1351680 | tf_op jit(solution)/shard_map/all_gather | solution.py:37
  413.9 127.8 %copy-start.2 = (bf16[4,640,160]{1,2,0:T(8,128)(2,1)S(1)}, bf16[4,640,160]{1,2,0:T(8,128)(2,1)}, u32[]{:S(2)}) copy-start(bf16[4,640,160]{1,2,0:T(8,128)(2,1)} %param.7) | copy-start | bytes 2457604
  434.2 428.5 %reduce-scatter.9.cloned.1.call-start = ((), (), s32[]{:S(2)}) async-start(), calls=%async_computation.10 | async-start | bytes 1351680
  545.5 482.8 %reduce-scatter.7.cloned.1.call-start = ((), (), s32[]{:S(2)}) async-start(), calls=%async_computation.9 | async-start | bytes 1351680
  865.2 165.5 %all-to-all-start.3 = ((bf16[32,2,320]{2,1,0:T(2,128)(2,1)}), bf16[32,2,320]{2,1,0:T(2,128)(2,1)S(1)}, u32[]{:S(2)}, u32[]{:S(2)}) async-start(bf16[32,2,320]{2,1,0:T(2,128)(2,1)} %reshape.24), calls=%async_computation.3 | async-start | bytes 98304 | tf_op jit(solution)/shard_map/all_to_all | solution.py:61
  1030.8 51.6 %all-to-all-start.2 = ((bf16[32,2,320]{2,1,0:T(2,128)(2,1)}), bf16[32,2,320]{2,1,0:T(2,128)(2,1)S(1)}, u32[]{:S(2)}, u32[]{:S(2)}) async-start(bf16[32,2,320]{2,1,0:T(2,128)(2,1)} %reshape.22), calls=%async_computation.2 | async-start | bytes 98304 | tf_op jit(solution)/shard_map/all_to_all | solution.py:64
  1067.8 369.3 %all-reduce.7.cloned.1.call-start = ((), (), s32[]{:S(2)}) async-start(), calls=%async_computation.11 | async-start | bytes 4194304 | tf_op jit(solution)/shard_map/psum | solution.py:70
  1085.3 1.3 copy-start.1
  1086.6 1.3 copy-start.8
  1087.9 1.4 copy-start.5
  1437.1 2.3 copy-start.9
Sparse Core Ops, SparseCore 0:
  11.5 367.4 all-reduce.4
  413.0 128.6 all-gather.4
  545.3 153.4 all-gather.2
  702.4 160.2 reduce-scatter.8
  866.0 162.2 reduce-scatter.6
  1085.4 351.6 all-reduce.6
where the time goes:
time: 1460 us
  waiting for transfers between devices  1180 us (81%)
  blocking collectives  146 us (10%)
  starting transfers between devices  74.9 us (5%)
  matrix products  16.4 us (1%)
  other arithmetic  16.4 us (1%)
  local copies, waits for them, and re-layouts  16.1 us (1%)
    psum x1, waiting for transfers between devices, local(): dcomb, ddisp = lax.psum((dcomb, ddisp), 'expert')  347 us
    unnamed x8, waiting for transfers between devices  286 us
    psum x1, waiting for transfers between devices, local(): prod, row_sq, col_sq = lax.psum((prod, row_sq, col_sq), 'expert')  270 us
    all_gather x1, waiting for transfers between devices, local(): lax.all_gather(grads, 'dp', axis=0, tiled=True)  153 us
    all_gather x1, waiting for transfers between devices, local(): lax.all_gather(rows, 'dp', axis=0, tiled=True)  107 us
    psum x1, blocking collectives, local(): prod, row_sq, col_sq = lax.psum((prod, row_sq, col_sq), 'expert')  99.7 us
    all_to_all x1, starting transfers between devices, local(): lax.all_to_all(summed_out.astype(jnp.bfloat16), 'expert', split_axis=2, c...  37.4 us
    all_to_all x1, starting transfers between devices, local(): lax.all_to_all(summed_back.astype(jnp.bfloat16), 'expert', split_axis=2,...  37.1 us
  transfers between devices with their start and end apart: 8, of which 7 were waited for; matrix products, arithmetic and copies ran while one was open for 1% of the time, Pallas kernels for 0%

commit v1 on v0

v1 whole, which is shorter than its diff:
```python
import functools

import jax
import jax.numpy as jnp
from jax import lax
from jax.experimental import pallas as pl
from jax.experimental.pallas import tpu as pltpu
from jax.sharding import PartitionSpec as P

SCALE = 32.0
EPS = 1e-06
MESH = pl.DeviceIdType.MESH
BF = jnp.bfloat16
F32 = jnp.float32
NZ, NY = 4, 8


def spread_kernel(n, per, x_ref, y_ref, local_sem, send_sem, recv_sem):
    me = lax.axis_index("expert")
    barrier = pltpu.get_barrier_semaphore()

    def greet(k, carry):
        pl.semaphore_signal(
            barrier, inc=1, device_id={"expert": lax.rem(me + k, n)}, device_id_type=MESH
        )
        return carry

    def copy(k):
        to = lax.rem(me + k, n)
        return pltpu.make_async_remote_copy(
            src_ref=x_ref.at[lax.div(to, per)],
            dst_ref=y_ref.at[me],
            send_sem=send_sem.at[k],
            recv_sem=recv_sem.at[k],
            device_id={"expert": to},
            device_id_type=MESH,
        )

    def start(k, carry):
        copy(k).start()
        return carry

    def finish(k, carry):
        copy(k).wait()
        return carry

    lax.fori_loop(1, n, greet, 0)
    own = pltpu.make_async_copy(x_ref.at[lax.div(me, per)], y_ref.at[me], local_sem)
    own.start()
    pl.semaphore_wait(barrier, n - 1)
    lax.fori_loop(1, n, start, 0)
    own.wait()
    lax.fori_loop(1, n, finish, 0)


def spread(x, n, per, collective_id):
    return pl.pallas_call(
        functools.partial(spread_kernel, n, per),
        out_shape=jax.ShapeDtypeStruct((n,) + x.shape[1:], x.dtype),
        in_specs=[pl.BlockSpec(memory_space=pltpu.VMEM)],
        out_specs=pl.BlockSpec(memory_space=pltpu.VMEM),
        scratch_shapes=[
            pltpu.SemaphoreType.DMA,
            pltpu.SemaphoreType.DMA((n,)),
            pltpu.SemaphoreType.DMA((n,)),
        ],
        compiler_params=pltpu.CompilerParams(
            collective_id=collective_id, has_side_effects=True, vmem_limit_bytes=24 * 2**20
        ),
    )(x)


def place():
    p = lax.axis_index("dp")
    return lax.div(p, NY), lax.rem(p, NY)


def at(z, y):
    return lax.rem(z, NZ) * NY + lax.rem(y, NY)


def greet_grid(z, y):
    barrier = pltpu.get_barrier_semaphore()
    others = [at(z, y + 1), at(z, y + NY - 1)] + [at(z + k, y) for k in range(1, NZ)]
    for other in others:
        pl.semaphore_signal(barrier, inc=1, device_id={"dp": other}, device_id_type=MESH)
    pl.semaphore_wait(barrier, len(others))


def gather_kernel(b_ref, y_ref, local_sem, z_send, z_recv, y_send, y_recv):
    z, y = place()
    p = at(z, y)
    greet_grid(z, y)
    own = pltpu.make_async_copy(b_ref, y_ref.at[:, p], local_sem)
    own.start()

    def z_copy(k):
        return pltpu.make_async_remote_copy(
            src_ref=b_ref,
            dst_ref=y_ref.at[:, p],
            send_sem=z_send.at[k],
            recv_sem=z_recv.at[k],
            device_id={"dp": at(z + k, y)},
            device_id_type=MESH,
        )

    def y_copy(chain, step, way):
        back = NY - (step - 1) if way == 0 else step - 1
        slot = at(z + chain, y + back)
        rows = pl.ds(0, 8) if step < NY // 2 else pl.ds(4 * way, 4)
        src = b_ref if chain == 0 and step == 1 else y_ref.at[:, slot]
        return pltpu.make_async_remote_copy(
            src_ref=src.at[rows],
            dst_ref=y_ref.at[rows, slot],
            send_sem=y_send.at[chain, step, way],
            recv_sem=y_recv.at[chain, step, way],
            device_id={"dp": at(z, y + (1 if way == 0 else NY - 1))},
            device_id_type=MESH,
        )

    z_copies = {k: z_copy(k) for k in (3, 1, 2)}
    y_copies = {}
    for way in (0, 1):
        y_copies[0, 1, way] = y_copy(0, 1, way)
        y_copies[0, 1, way].start()
    for k in (3, 1, 2):
        z_copies[k].start()
    for chain in (1, 3, 2):
        z_copies[NZ - chain].wait_recv()
        for way in (0, 1):
            y_copies[chain, 1, way] = y_copy(chain, 1, way)
            y_copies[chain, 1, way].start()
    for step in range(2, NY // 2 + 1):
        for chain in (0, 1, 3, 2):
            for way in (0, 1):
                y_copies[chain, step - 1, way].wait_recv()
                y_copies[chain, step, way] = y_copy(chain, step, way)
                y_copies[chain, step, way].start()
    for chain in (0, 1, 3, 2):
        for way in (0, 1):
            y_copies[chain, NY // 2, way].wait_recv()
    own.wait()
    for copy in z_copies.values():
        copy.wait_send()
    for copy in y_copies.values():
        copy.wait_send()


def gather(block, collective_id):
    a, j, d = block.shape
    return pl.pallas_call(
        gather_kernel,
        out_shape=jax.ShapeDtypeStruct((a, NZ * NY, j, d), block.dtype),
        in_specs=[pl.BlockSpec(memory_space=pltpu.VMEM)],
        out_specs=pl.BlockSpec(memory_space=pltpu.VMEM),
        scratch_shapes=[
            pltpu.SemaphoreType.DMA,
            pltpu.SemaphoreType.DMA((NZ,)),
            pltpu.SemaphoreType.DMA((NZ,)),
            pltpu.SemaphoreType.DMA((NZ, NY // 2 + 1, 2)),
            pltpu.SemaphoreType.DMA((NZ, NY // 2 + 1, 2)),
        ],
        compiler_params=pltpu.CompilerParams(
            collective_id=collective_id, has_side_effects=True, vmem_limit_bytes=32 * 2**20
        ),
    )(block)


def scatter_kernel(p_ref, o_ref, ring, total, z_out, z_in, z_send, z_recv, y_send, y_recv):
    z, y = place()
    greet_grid(z, y)
    half = NY // 2

    def y_copy(chain, step, way):
        slot = at(z + chain, y + (step if way == 0 else NY - step))
        rows = pl.ds(4 * way, 4) if step == half else pl.ds(0, 8)
        src = p_ref.at[:, slot] if step == half else ring.at[chain, step, way]
        return pltpu.make_async_remote_copy(
            src_ref=src.at[rows],
            dst_ref=ring.at[chain, step - 1, way, rows],
            send_sem=y_send.at[chain, step, way],
            recv_sem=y_recv.at[chain, step, way],
            device_id={"dp": at(z, y + (1 if way == 0 else NY - 1))},
            device_id_type=MESH,
        )

    def z_copy(chain):
        return pltpu.make_async_remote_copy(
            src_ref=z_out.at[chain],
            dst_ref=z_in.at[chain],
            send_sem=z_send.at[chain],
            recv_sem=z_recv.at[chain],
            device_id={"dp": at(z + chain, y)},
            device_id_type=MESH,
        )

    order = (1, 3, 2, 0)
    y_copies, z_copies = {}, {}
    for chain in order:
        for way in (0, 1):
            y_copies[chain, half, way] = y_copy(chain, half, way)
            y_copies[chain, half, way].start()
    for step in range(half - 1, 0, -1):
        for chain in order:
            for way in (0, 1):
                y_copies[chain, step + 1, way].wait_recv()
                slot = at(z + chain, y + (step if way == 0 else NY - step))
                for a in range(8):
                    mine = p_ref[a, slot]
                    if step < half - 1 or a // 4 == way:
                        mine = (mine.astype(F32) + ring[chain, step, way, a].astype(F32)).astype(BF)
                    ring[chain, step, way, a] = mine
                y_copies[chain, step, way] = y_copy(chain, step, way)
                y_copies[chain, step, way].start()
    here = [at(z + chain, y) for chain in range(NZ)]
    for chain in order:
        for way in (0, 1):
            y_copies[chain, 1, way].wait_recv()
        for a in range(8):
            summed = (
                p_ref[a, here[chain]].astype(F32)
                + ring[chain, 0, 0, a].astype(F32)
                + ring[chain, 0, 1, a].astype(F32)
            )
            if chain == 0:
                total[a] = summed
            else:
                z_out[chain, a] = summed.astype(BF)
        if chain != 0:
            z_copies[chain] = z_copy(chain)
            z_copies[chain].start()
    for chain in (1, 3, 2):
        z_copies[chain].wait_recv()
    for a in range(8):
        o_ref[a] = (
            total[a]
            + z_in[1, a].astype(F32)
            + z_in[2, a].astype(F32)
            + z_in[3, a].astype(F32)
        )
    for copy in z_copies.values():
        copy.wait_send()
    for copy in y_copies.values():
        copy.wait_send()


def scatter(parts, collective_id):
    a, _, j, d = parts.shape
    return pl.pallas_call(
        scatter_kernel,
        out_shape=jax.ShapeDtypeStruct((a, j, d), F32),
        in_specs=[pl.BlockSpec(memory_space=pltpu.VMEM)],
        out_specs=pl.BlockSpec(memory_space=pltpu.VMEM),
        scratch_shapes=[
            pltpu.VMEM((NZ, NY // 2, 2, a, j, d), BF),
            pltpu.VMEM((a, j, d), F32),
            pltpu.VMEM((NZ, a, j, d), BF),
            pltpu.VMEM((NZ, a, j, d), BF),
            pltpu.SemaphoreType.DMA((NZ,)),
            pltpu.SemaphoreType.DMA((NZ,)),
            pltpu.SemaphoreType.DMA((NZ, NY // 2 + 1, 2)),
            pltpu.SemaphoreType.DMA((NZ, NY // 2 + 1, 2)),
        ],
        compiler_params=pltpu.CompilerParams(
            collective_id=collective_id, has_side_effects=True, vmem_limit_bytes=40 * 2**20
        ),
    )(parts)


def three(x):
    hi = lax.reduce_precision(x, 8, 7)
    mid = lax.reduce_precision(x - hi, 8, 7)
    low = x - hi - mid
    packed = jnp.stack([hi, mid, low], -1).astype(BF)
    return jnp.pad(packed, [(0, 0)] * x.ndim + [(0, 125)])


def joined(packed):
    return packed[..., 0].astype(F32) + packed[..., 1].astype(F32) + packed[..., 2].astype(F32)


def local(n, tokens, slot_params, w_in, w_out, out_grad):
    images, patches, feats = tokens.shape
    per = n // images
    m = patches // per
    slots = slot_params.shape[1]
    d = n * feats
    own = slots // n

    def cut(x):
        return jnp.transpose(x.reshape(images, per, m, feats), (0, 1, 3, 2)).reshape(n, feats, m)

    packed = jnp.concatenate(
        [cut(tokens), cut(out_grad), jnp.broadcast_to(slot_params, (n, feats, slots))], 2
    )
    packed = spread(packed, n, 1, 0).reshape(d, 2 * m + slots)
    x, g, params = packed[:, :m], packed[:, m : 2 * m], packed[:, 2 * m :]

    xf = x.astype(F32)
    pf = params.astype(F32)
    prod = jnp.einsum("dm,ds->ms", x, params, preferred_element_type=F32)
    row_inv = lax.rsqrt(jnp.sum(xf * xf, 0) + EPS)
    col_inv = lax.rsqrt(jnp.sum(pf * pf, 0) + EPS)
    logits = SCALE * prod * row_inv[:, None] * col_inv[None, :]
    expo = jnp.exp(logits)
    combine = expo / jnp.sum(expo, 1, keepdims=True)
    part_in = jnp.einsum("ms,dm->sd", expo.astype(BF), x, preferred_element_type=F32)
    part_grad = jnp.einsum("ms,dm->sd", combine.astype(BF), g, preferred_element_type=F32)
    part_den = jnp.sum(expo, 0)

    rows = jnp.concatenate([part_in.astype(BF), three(part_den)], 1).reshape(n, own, d + 128)
    grads = jnp.pad(part_grad.astype(BF), [(0, 0), (0, 128)]).reshape(n, own, d + 128)
    parts = spread(jnp.concatenate([rows, grads], 1), n, 1, 1)
    parts = parts.reshape(images, per, 2 * own, d + 128)
    den = jnp.sum(joined(parts[:, :, :own, d:]), 1)
    sums = jnp.sum(parts[..., :d].astype(F32), 1)
    slot_in = jnp.transpose(sums[:, :own] / den[:, :, None], (1, 0, 2))
    slot_grad = jnp.transpose(sums[:, own:], (1, 0, 2))
    block = jnp.concatenate([slot_in, slot_grad], 0).astype(BF)

    every = gather(block, 2).reshape(2 * own, -1, d)
    xs, gs = every[:own], every[own:]
    hidden = jnp.einsum("end,edf->enf", xs, w_in, preferred_element_type=F32)
    act_b = jax.nn.gelu(hidden).astype(BF)
    out_part = jnp.einsum("enf,efd->end", act_b, w_out, preferred_element_type=F32)
    dact = jnp.einsum("end,efd->enf", gs, w_out, preferred_element_type=F32)
    _, pull = jax.vjp(jax.nn.gelu, hidden)
    dhid = pull(dact)[0].astype(BF)
    back_part = jnp.einsum("enf,edf->end", dhid, w_in, preferred_element_type=F32)
    summed = jnp.concatenate([out_part.astype(BF), back_part.astype(BF)], 0)
    summed = scatter(summed.reshape(2 * own, -1, images, d), 3)
    grad_w_out = jnp.einsum("enf,end->efd", act_b, gs, preferred_element_type=F32).astype(BF)
    grad_w_in = jnp.einsum("end,enf->edf", xs, dhid, preferred_element_type=F32).astype(BF)

    summed = jnp.transpose(summed, (1, 0, 2))
    slot_back = summed[:, own:].astype(BF)
    mean = jnp.sum(jnp.transpose(slot_in, (1, 0, 2)) * slot_back.astype(F32), 2)
    extra = three(jnp.concatenate([1.0 / den, mean], 1))
    results = jnp.concatenate([summed.astype(BF), extra], 2)
    results = spread(results, n, per, 4)
    slot_out = results[:, :own, :d].reshape(slots, d)
    slot_back = results[:, own:, :d].reshape(slots, d)
    den_inv = joined(results[:, :own, d:]).reshape(slots)
    mean = joined(results[:, own:, d:]).reshape(slots)

    dispatch = expo * den_inv[None, :]
    dcomb = jnp.einsum("dm,sd->ms", g, slot_out, preferred_element_type=F32)
    ddisp = jnp.einsum("dm,sd->ms", x, slot_back, preferred_element_type=F32)
    dlog = combine * (dcomb - jnp.sum(combine * dcomb, 1, keepdims=True))
    dlog = dlog + dispatch * (ddisp - mean[None, :])
    centre = jnp.sum(dlog * logits, 1)
    pulled = (SCALE * dlog * col_inv[None, :]).astype(BF)
    backward = jnp.einsum("ms,ds->dm", pulled, params, preferred_element_type=F32)
    direct = jnp.einsum("ms,sd->dm", dispatch.astype(BF), slot_back, preferred_element_type=F32)
    grad = direct + row_inv[None, :] * (backward - xf * (row_inv * centre)[None, :])
    grad = spread(grad.astype(BF).reshape(n, feats, m), n, 1, 5)
    grad = jnp.transpose(grad.reshape(images, per, feats, m), (0, 1, 3, 2))
    return (grad.reshape(images, patches, feats), grad_w_in, grad_w_out)


def solution(mesh):
    return jax.shard_map(
        functools.partial(local, mesh.shape["expert"]),
        mesh=mesh,
        in_specs=(
            P("dp", None, "expert"),
            P("expert", None),
            P("expert", None, "dp"),
            P("expert", "dp", None),
            P("dp", None, "expert"),
        ),
        out_specs=(P("dp", None, "expert"), P("expert", None, "dp"), P("expert", "dp", None)),
        check_vma=False,
    )
```

time: 1460 us -> 206 us (0.14)
  waiting for transfers between devices: 1180 us -> 0 us
  Pallas kernels: 0 us -> 191 us
  blocking collectives: 146 us -> 0 us
  starting transfers between devices: 74.9 us -> 0 us
    psum x2 -> x0, waiting for transfers between devices: 617 us -> none  [the longest x1 347 us: local(): dcomb, ddisp = lax.psum((dcomb, ddisp), 'expert')]
    unnamed x8 -> x0, waiting for transfers between devices: 286 us -> none
    all_gather x2 -> x0, waiting for transfers between devices: 261 us -> none  [the longest x1 153 us: local(): lax.all_gather(grads, 'dp', axis=0, tiled=True)]
    pallas_call x0 -> x6, Pallas kernels: none -> 191 us  [the longest x4 110 us: spread(): pl.pallas_call(functools.partial(spread_kernel, n, per), out_shape=jax.Sh...]
    psum x1 -> x0, blocking collectives: 99.7 us -> none  [local(): prod, row_sq, col_sq = lax.psum((prod, row_sq, col_sq), 'expert')]
    all_to_all x2 -> x0, starting transfers between devices: 74.4 us -> none  [the longest x1 37.4 us: local(): lax.all_to_all(summed_out.astype(jnp.bfloat16), 'expert', split_axis=2, c...]
    all_to_all x2 -> x0, blocking collectives: 46.5 us -> none  [the longest x1 28.2 us: local(): lax.all_to_all(slot_in, 'expert', split_axis=1, concat_axis=2, tiled=True)]
  transfers between devices with their start and end apart: 8 -> 0, of which waited for: 7 -> 0; matrix products, arithmetic and copies ran while one was open for 1% -> 0% of each run, Pallas kernels for 0% -> 0%
where the time goes in v1:
time: 206 us
  Pallas kernels  191 us (93%)
  matrix products  7.25 us (4%)
  local copies, waits for them, and re-layouts  5.18 us (3%)
    pallas_call x4, Pallas kernels, spread(): pl.pallas_call(functools.partial(spread_kernel, n, per), out_shape=jax.Sh...  110 us
    pallas_call x1, Pallas kernels, gather(): pl.pallas_call(gather_kernel, out_shape=jax.ShapeDtypeStruct((a, NZ * NY,...  49.6 us
    pallas_call x1, Pallas kernels, scatter(): pl.pallas_call(scatter_kernel, out_shape=jax.ShapeDtypeStruct((a, j, d),...  31.4 us

profile of v1, /device:TPU:1, one launch (start us, length us, event | category | flops | bytes accessed | tf_op | source)
XLA Modules:
  0.0 205.9 jit_solution(7496503490312108757)
XLA Ops:
  0.6 0.0 copy-start
  0.6 1.1 reshape.219
  1.7 0.1 copy.32
  1.8 1.0 reshape.221
  2.9 0.1 copy.33
  2.9 0.7 broadcast_in_dim.2
  3.6 0.2 pad_maximum_fusion.x_ref
  3.9 32.8 %shard_map.76 = bf16[32,20,256]{2,1,0:T(8,128)(2,1)S(1)} custom-call(bf16[32,20,256]{2,1,0:T(8,128)(2,1)S(1)} %pad_maximum_fusion.x_ref), custom_call_target="tpu_custom_call" | custom-call | tf_op jit(solution)/shard_map/pallas_call | solution.py:57
  36.6 0.1 reshape.223
  36.7 0.1 multiply_reduce_fusion
  36.9 0.1 copy.47
  37.0 0.1 fusion.27
  37.1 0.3 exponential_reduce_fusion.1
  37.5 0.1 copy.35
  37.6 0.3 convolution_convert_fusion.4
  38.0 0.1 reshape.225
  38.0 0.2 convolution_convert_fusion.5
  38.3 0.1 reshape.224
  38.3 0.2 pad_maximum_fusion.1.x_ref
  38.5 20.9 %shard_map.77 = bf16[32,8,768]{2,1,0:T(8,128)(2,1)S(1)} custom-call(bf16[32,8,768]{2,1,0:T(8,128)(2,1)S(1)} %pad_maximum_fusion.1.x_ref), custom_call_target="tpu_custom_call" | custom-call | tf_op jit(solution)/shard_map/pallas_call | solution.py:57
  59.5 0.2 add_reduce_fusion.2
  59.7 0.0 copy-start.1
  59.7 0.1 convert_bitcast_fusion
  59.9 49.6 %shard_map.78 = bf16[8,32,8,640]{3,2,1,0:T(8,128)(2,1)S(1)} custom-call(bf16[8,8,640]{2,1,0:T(8,128)(2,1)S(1)} %copy.36.b_ref), custom_call_target="tpu_custom_call" | custom-call | tf_op jit(solution)/shard_map/pallas_call | solution.py:151
  109.5 0.0 copy-done.1
  109.6 0.6 fusion.4
  110.1 0.0 copy-done
  110.2 0.8 fusion.21
  110.9 1.3 convolution_convert_fusion.2
  112.2 1.4 convolution_convert_fusion.3
  113.6 0.6 convolution_convert_fusion.1
  114.2 0.6 convolution_convert_fusion
  114.9 0.3 maximum_bitcast_fusion.p_ref
  115.2 31.4 %shard_map.79 = f32[8,8,640]{2,1,0:T(8,128)S(1)} custom-call(bf16[8,32,8,640]{3,2,1,0:T(8,128)(2,1)S(1)} %maximum_bitcast_fusion.p_ref), custom_call_target="tpu_custom_call" | custom-call | tf_op jit(solution)/shard_map/pallas_call | solution.py:249
  146.6 0.2 multiply_reduce_fusion.1
  146.7 0.1 reduce-precision_convert_fusion.1
  146.8 0.1 copy.42
  147.0 32.1 %shard_map.80 = bf16[32,8,768]{2,1,0:T(8,128)(2,1)S(1)} custom-call(bf16[8,8,768]{2,1,0:T(8,128)(2,1)S(1)} %fusion.33.x_ref), custom_call_target="tpu_custom_call" | custom-call | tf_op jit(solution)/shard_map/pallas_call | solution.py:57
  179.1 0.2 add_reduce_fusion.1
  179.4 0.1 fusion.45
  179.6 0.4 multiply_reduce_fusion.3
  180.0 0.1 add.102
  180.1 0.1 add.105
  180.2 0.3 multiply_reduce_fusion.2
  180.6 0.2 fusion.10
  180.8 0.2 fusion.11
  181.0 0.2 copy.43
  181.1 0.1 reshape.230.x_ref
  181.2 23.8 %shard_map.81 = bf16[32,20,64]{2,1,0:T(8,128)(2,1)S(1)} custom-call(bf16[32,20,64]{2,1,0:T(8,128)(2,1)S(1)} %reshape.230.x_ref), custom_call_target="tpu_custom_call" | custom-call | tf_op jit(solution)/shard_map/pallas_call | solution.py:57
  205.0 0.1 copy.44
  205.1 0.8 reshape.232
  (18 shorter events, 0.4 us)
Async XLA Ops:
  0.6 109.5 %copy-start = (bf16[4,160,640]{2,1,0:T(8,128)(2,1)S(1)}, bf16[4,160,640]{2,1,0:T(8,128)(2,1)}, u32[]{:S(2)}) copy-start(bf16[4,160,640]{2,1,0:T(8,128)(2,1)} %param.8) | copy-start | bytes 2457604
  59.7 49.9 %copy-start.1 = (bf16[4,640,160]{1,2,0:T(8,128)(2,1)S(1)}, bf16[4,640,160]{1,2,0:T(8,128)(2,1)}, u32[]{:S(2)}) copy-start(bf16[4,640,160]{1,2,0:T(8,128)(2,1)} %param.7) | copy-start | bytes 2457604

commit v2 on v0

v2 whole, which is shorter than its diff:
```python
import functools

import jax
import jax.numpy as jnp
from jax import lax
from jax.experimental import pallas as pl
from jax.experimental.pallas import tpu as pltpu
from jax.sharding import PartitionSpec as P

SCALE = 32.0
EPS = 1e-06
MESH = pl.DeviceIdType.MESH
BF = jnp.bfloat16
F32 = jnp.float32
NZ, NY = 4, 8
NE = 32
IM = NE // 4
D = 640
EXTRA = 128
NT = (((1,), (1,)), ((), ()))
TN = (((0,), (0,)), ((), ()))


def mm(a, b, dims=(((1,), (0,)), ((), ()))):
    return lax.dot_general(a, b, dims, preferred_element_type=F32)


def at(z, y):
    return lax.rem(z, NZ) * NY + lax.rem(y, NY)


def team(j, q):
    return lax.rem(j, IM) * 4 + lax.rem(q, 4)


def send(src, dst, send_sem, recv_sem, **to):
    copy = pltpu.make_async_remote_copy(
        src_ref=src,
        dst_ref=dst,
        send_sem=send_sem,
        recv_sem=recv_sem,
        device_id=to,
        device_id_type=MESH,
    )
    return copy


def three(x, lane, first):
    hi = x.astype(BF).astype(F32)
    mid = (x - hi).astype(BF).astype(F32)
    low = x - hi - mid
    zero = jnp.zeros_like(x)
    return jnp.where(
        lane == first,
        hi,
        jnp.where(lane == first + 1, mid, jnp.where(lane == first + 2, low, zero)),
    )


def greet(me, z, y):
    barrier = pltpu.get_barrier_semaphore()

    def one(k, carry):
        pl.semaphore_signal(
            barrier, inc=1, device_id={"expert": lax.rem(me + k, NE)}, device_id_type=MESH
        )
        return carry

    lax.fori_loop(1, NE, one, 0)
    others = [at(z, y + 1), at(z, y + NY - 1)] + [at(z + k, y) for k in range(1, NZ)]
    for other in others:
        pl.semaphore_signal(barrier, inc=1, device_id={"dp": other}, device_id_type=MESH)
    pl.semaphore_wait(barrier, NE - 1 + len(others))


def spread(x_ref, y_ref, sems):
    me = lax.axis_index("expert")
    send_sem, recv_sem = sems

    def copy(k):
        to = lax.rem(me + k, NE)
        return send(x_ref.at[to], y_ref.at[me], send_sem.at[k], recv_sem.at[k], expert=to)

    def start(k, carry):
        copy(k).start()
        return carry

    def finish(k, carry):
        copy(k).wait()
        return carry

    lax.fori_loop(1, NE, start, 0)
    y_ref[me] = x_ref[me]
    return lambda: lax.fori_loop(1, NE, finish, 0)


def share_along(w_ref, v_ref, sems):
    me = lax.axis_index("expert")
    hi, lo = lax.div(me, 8), lax.rem(me, 8)
    copies = []
    for k in range(1, 4):
        to = lax.rem(hi + k, 4) * 8 + lo
        copies.append(
            send(w_ref, v_ref.at[hi, lo], sems[0].at[k], sems[1].at[k], expert=to)
        )
        copies[-1].start()
    v_ref[hi, lo] = w_ref[...]
    return copies


def share_across(v_ref, sems):
    me = lax.axis_index("expert")
    hi, lo = lax.div(me, 8), lax.rem(me, 8)
    copies = []
    for k in range(1, 8):
        to = hi * 8 + lax.rem(lo + k, 8)
        copies.append(
            send(v_ref.at[:, lo], v_ref.at[:, lo], sems[0].at[k], sems[1].at[k], expert=to)
        )
        copies[-1].start()
    return copies


def collect(x_ref, o_ref, part, total, q_sems, j_sems):
    me = lax.axis_index("expert")
    j, q = lax.div(me, 4), lax.rem(me, 4)
    q_copies, j_copies = {}, {}
    steps = list(range(1, IM)) + [0]
    for step in steps:
        to = lax.rem(j + step, IM)
        for k in range(1, 4):
            q_copies[step, k] = send(
                x_ref.at[lax.rem(q + k, 4), to],
                part.at[k, step],
                q_sems[0].at[step, k],
                q_sems[1].at[step, k],
                expert=team(j, q + k),
            )
            q_copies[step, k].start()
    for step in steps:
        to = lax.rem(j + step, IM)
        for k in range(1, 4):
            q_copies[step, k].wait_recv()
        summed = x_ref[q, to].astype(F32)
        for k in range(1, 4):
            summed = summed + part[k, step].astype(F32)
        if step == 0:
            o_ref[j] = summed.astype(BF)
            continue
        total[step] = summed.astype(BF)
        j_copies[step] = send(
            total.at[step],
            o_ref.at[j],
            j_sems[0].at[step],
            j_sems[1].at[step],
            expert=team(to, q),
        )
        j_copies[step].start()
    for copy in j_copies.values():
        copy.wait()
    for copy in q_copies.values():
        copy.wait_send()


def give_back(x_ref, o_ref, q_sems, j_sems):
    me = lax.axis_index("expert")
    j, q = lax.div(me, 4), lax.rem(me, 4)
    q_copies, j_copies = {}, {}
    for step in range(1, IM):
        to = lax.rem(j + step, IM)
        j_copies[step] = send(
            x_ref.at[to],
            o_ref.at[q, j],
            j_sems[0].at[step],
            j_sems[1].at[step],
            expert=team(to, q),
        )
        j_copies[step].start()
    o_ref[q, j] = x_ref[j]
    for step in range(IM):
        here = lax.rem(j + IM - step, IM)
        if step:
            j_copies[step].wait_recv()
        for k in range(1, 4):
            q_copies[step, k] = send(
                o_ref.at[q, here],
                o_ref.at[q, here],
                q_sems[0].at[step, k],
                q_sems[1].at[step, k],
                expert=team(j, q + k),
            )
            q_copies[step, k].start()
    for copy in q_copies.values():
        copy.wait()
    for copy in j_copies.values():
        copy.wait_send()


def gather(b_ref, y_ref, z, y, z_sems, y_sems):
    p = at(z, y)

    def y_copy(chain, step, way):
        back = NY - (step - 1) if way == 0 else step - 1
        slot = at(z + chain, y + back)
        rows = pl.ds(0, 8) if step < NY // 2 else pl.ds(4 * way, 4)
        src = b_ref if chain == 0 and step == 1 else y_ref.at[:, slot]
        return send(
            src.at[rows],
            y_ref.at[rows, slot],
            y_sems[0].at[chain, step, way],
            y_sems[1].at[chain, step, way],
            dp=at(z, y + (1 if way == 0 else NY - 1)),
        )

    y_copies, z_copies = {}, {}
    for way in (0, 1):
        y_copies[0, 1, way] = y_copy(0, 1, way)
        y_copies[0, 1, way].start()
    for k in (3, 1, 2):
        z_copies[k] = send(
            b_ref, y_ref.at[:, p], z_sems[0].at[k], z_sems[1].at[k], dp=at(z + k, y)
        )
        z_copies[k].start()
    y_ref[:, p] = b_ref[...]
    for chain in (1, 3, 2):
        z_copies[NZ - chain].wait_recv()
        for way in (0, 1):
            y_copies[chain, 1, way] = y_copy(chain, 1, way)
            y_copies[chain, 1, way].start()
    for step in range(2, NY // 2 + 1):
        for chain in (0, 1, 3, 2):
            for way in (0, 1):
                y_copies[chain, step - 1, way].wait_recv()
                y_copies[chain, step, way] = y_copy(chain, step, way)
                y_copies[chain, step, way].start()
    for chain in (0, 1, 3, 2):
        for way in (0, 1):
            y_copies[chain, NY // 2, way].wait_recv()
    for copy in z_copies.values():
        copy.wait_send()
    for copy in y_copies.values():
        copy.wait_send()


def scatter(p_ref, total, ring, z_out, z_in, z, y, z_sems, y_sems, meanwhile):
    half = NY // 2

    def y_copy(chain, step, way):
        slot = at(z + chain, y + (step if way == 0 else NY - step))
        rows = pl.ds(4 * way, 4) if step == half else pl.ds(0, 8)
        src = p_ref.at[:, slot] if step == half else ring.at[chain, step, way]
        return send(
            src.at[rows],
            ring.at[chain, step - 1, way, rows],
            y_sems[0].at[chain, step, way],
            y_sems[1].at[chain, step, way],
            dp=at(z, y + (1 if way == 0 else NY - 1)),
        )

    order = (1, 3, 2, 0)
    y_copies, z_copies = {}, {}
    for chain in order:
        for way in (0, 1):
            y_copies[chain, half, way] = y_copy(chain, half, way)
            y_copies[chain, half, way].start()
    meanwhile()
    for step in range(half - 1, 0, -1):
        for chain in order:
            for way in (0, 1):
                y_copies[chain, step + 1, way].wait_recv()
                slot = at(z + chain, y + (step if way == 0 else NY - step))
                for a in range(8):
                    mine = p_ref[a, slot]
                    if step < half - 1 or a // 4 == way:
                        mine = (mine.astype(F32) + ring[chain, step, way, a].astype(F32)).astype(BF)
                    ring[chain, step, way, a] = mine
                y_copies[chain, step, way] = y_copy(chain, step, way)
                y_copies[chain, step, way].start()
    for chain in order:
        for way in (0, 1):
            y_copies[chain, 1, way].wait_recv()
        here = at(z + chain, y)
        for a in range(8):
            summed = (
                p_ref[a, here].astype(F32)
                + ring[chain, 0, 0, a].astype(F32)
                + ring[chain, 0, 1, a].astype(F32)
            )
            if chain == 0:
                total[a] = summed
            else:
                z_out[chain, a] = summed.astype(BF)
        if chain != 0:
            z_copies[chain] = send(
                z_out.at[chain],
                z_in.at[chain],
                z_sems[0].at[chain],
                z_sems[1].at[chain],
                dp=at(z + chain, y),
            )
            z_copies[chain].start()
    for chain in (1, 3, 2):
        z_copies[chain].wait_recv()
    for a in range(8):
        total[a] = (
            total[a]
            + z_in[1, a].astype(F32)
            + z_in[2, a].astype(F32)
            + z_in[3, a].astype(F32)
        )
    for copy in z_copies.values():
        copy.wait_send()
    for copy in y_copies.values():
        copy.wait_send()


def whole_kernel(
    x_ref, w_ref, win_ref, wout_ref,
    y_ref, gin_ref, gout_ref,
    xin, vin, xs, ps, parts, part, part_sum, sums, blk, blkb, every, outs, act_s, dhid_s,
    ring, z_out, z_in, total, res, resb, back, chunk,
    s1a, s1b, sa1, sa2, sb1, sb2, cq1, cq2, cj1, cj2, gz1, gz2, gy1, gy2,
    sz1, sz2, sy1, sy2, bq1, bq2, bj1, bj2, s2a, s2b,
):
    me = lax.axis_index("expert")
    quarter = lax.rem(me, 4)
    p = lax.axis_index("dp")
    z, y = lax.div(p, NY), lax.rem(p, NY)
    greet(me, z, y)

    along = share_along(w_ref, vin, (sa1, sa2))
    finish = spread(x_ref, xin, (s1a, s1b))
    for copy in along:
        copy.wait()
    across = share_across(vin, (sb1, sb2))
    finish()
    feats = xin.shape[1]
    for e in range(NE):
        xs[e * feats : (e + 1) * feats, :] = xin[e].astype(F32)
    both = xs[...].T
    both_b = both.astype(BF)
    m = both.shape[0] // 2
    for copy in across:
        copy.wait()
    for e in range(NE):
        ps[e * feats : (e + 1) * feats, :] = vin[e // 8, e % 8].astype(F32)
    params = ps[...]
    params_b = params.astype(BF)

    cols = 2 * NE * 4
    first = (lax.broadcasted_iota(jnp.int32, (1, cols), 1) & 4) == 0
    x = both[:m]
    row_inv = lax.rsqrt(jnp.sum(x * x, 1, keepdims=True) + EPS)
    col_inv = lax.rsqrt(jnp.sum(params * params, 0, keepdims=True) + EPS)
    logits = SCALE * mm(both_b[:m], params_b) * row_inv * col_inv
    expo = jnp.exp(logits)
    combine = expo / (0.5 * jnp.sum(expo, 1, keepdims=True))
    weights = jnp.concatenate([jnp.where(first, expo, 0.0), jnp.where(first, 0.0, combine)], 0).T
    slot_part = mm(weights.astype(BF), both_b)
    lane = lax.broadcasted_iota(jnp.int32, (cols, EXTRA), 1)
    upper = (lax.broadcasted_iota(jnp.int32, (cols, 1), 0) & 4) == 0
    den = jnp.where(upper, jnp.sum(weights, 1, keepdims=True), 0.0)
    den = three(den, lane, 32 * quarter)
    for e in range(NE):
        rows = slice(8 * e, 8 * e + 8)
        parts[e // IM, e % IM, :, :D] = slot_part[rows].astype(BF)
        parts[e // IM, e % IM, :, D:] = den[rows].astype(BF)
    collect(parts, sums, part, part_sum, (cq1, cq2), (cj1, cj2))

    top = lax.broadcasted_iota(jnp.int32, (8, 1), 0) < 4
    for j in range(IM):
        val = sums[j, :, :D].astype(F32)
        den = jnp.sum(sums[j, :, D:].astype(F32), 1, keepdims=True)
        val = val * jnp.where(top, 1.0 / den, 1.0)
        wide = jnp.broadcast_to(den, (8, EXTRA))
        for a in range(8):
            blk[a, j : j + 1, :D] = val[a : a + 1]
            blk[a, j : j + 1, D:] = wide[a : a + 1]
    for a in range(8):
        blkb[a] = blk[a, :, :D].astype(BF)
    gather(blkb, every, z, y, (gz1, gz2), (gy1, gy2))

    rows = NZ * NY * IM

    def merged(ref, a):
        return ref[a].astype(F32).reshape(rows, D).astype(BF)

    def forward(e, carry):
        xe, ge = merged(every, e), merged(every, 4 + e)
        hidden = mm(xe, win_ref[e], NT)
        act, pull = jax.vjp(jax.nn.gelu, hidden)
        act = act.astype(BF)
        dhid = pull(mm(ge, wout_ref[e], NT))[0].astype(BF)
        act_s[e] = act
        dhid_s[e] = dhid
        outs[e] = mm(act, wout_ref[e]).reshape(NZ * NY, IM, D).astype(BF)
        outs[4 + e] = mm(dhid, win_ref[e]).reshape(NZ * NY, IM, D).astype(BF)
        return carry

    def weight_grads(e, carry):
        gout_ref[e] = mm(act_s[e], merged(every, 4 + e), TN).astype(BF)
        gin_ref[e] = mm(dhid_s[e], merged(every, e), TN).astype(BF)
        return carry

    lax.fori_loop(0, 4, forward, 0)
    scatter(
        outs, total, ring, z_out, z_in, z, y, (sz1, sz2), (sy1, sy2),
        lambda: lax.fori_loop(0, 4, weight_grads, 0),
    )

    lane = lax.broadcasted_iota(jnp.int32, (8, EXTRA), 1)
    for a in range(8):
        val = total[a]
        if a < 4:
            extra = jnp.zeros((8, EXTRA), F32)
        else:
            mean = jnp.sum(blk[a - 4, :, :D] * val, 1, keepdims=True)
            extra = three(mean, lane, 0) + three(1.0 / blk[a - 4, :, D : D + 1], lane, 32)
        for j in range(IM):
            res[j, a : a + 1, :D] = val[j : j + 1]
            res[j, a : a + 1, D:] = extra[j : j + 1]
    for j in range(IM):
        resb[j] = res[j].astype(BF)
    give_back(resb, back, (bq1, bq2), (bj1, bj2))

    slots = back[...].astype(F32).reshape(cols, D + EXTRA).astype(BF)
    slot_rows, extra = slots[:, :D], slots[:, D:]
    which = lax.broadcasted_iota(jnp.int32, (8, EXTRA), 0)
    pick = (lax.broadcasted_iota(jnp.int32, (8, EXTRA), 1) >> 5) == which
    scalars = mm(jnp.where(pick, 1.0, 0.0).astype(BF), extra, NT)
    mean, den_inv = scalars[0:1], scalars[1:2]
    prods = mm(both_b, slot_rows, NT)
    dispatch = expo * den_inv
    taken = combine * prods[m:]
    dot = jnp.sum(jnp.where(first, taken, 0.0), 1, keepdims=True)
    dlog = jnp.where(first, taken - combine * dot, dispatch * (prods[:m] - mean))
    centre = jnp.sum(dlog * logits, 1, keepdims=True)
    pulled = (SCALE * dlog * col_inv).astype(BF)
    grad = mm(jnp.where(first, 0.0, dispatch).astype(BF), slot_rows)
    grad = grad + row_inv * (mm(pulled, params_b, NT) - x * (row_inv * centre))
    xs[...] = jnp.concatenate([grad, grad], 0).T
    low = lax.broadcasted_iota(jnp.int32, (1, 2 * m), 1) < m
    for e in range(NE):
        a, b, c = e * feats, e * feats + feats // 2, (e + 1) * feats
        chunk[e] = jnp.where(low, xs[a:b, :], xs[b:c, :]).astype(BF)
    spread(chunk, y_ref, (s2a, s2b))()


def whole(x, w, win, wout):
    _, feats, lanes = x.shape
    cols = w.shape[1]
    experts, f, d = win.shape
    dma = pltpu.SemaphoreType.DMA
    ring = dma((NZ, NY // 2 + 1, 2))

    def two(*shape):
        return [dma(shape), dma(shape)]

    block = (8, IM, d)
    return pl.pallas_call(
        whole_kernel,
        out_shape=(
            jax.ShapeDtypeStruct((NE, feats // 2, lanes), BF),
            jax.ShapeDtypeStruct(win.shape, BF),
            jax.ShapeDtypeStruct(win.shape, BF),
        ),
        in_specs=[pl.BlockSpec(memory_space=pltpu.VMEM)] * 4,
        out_specs=(pl.BlockSpec(memory_space=pltpu.VMEM),) * 3,
        scratch_shapes=[
            pltpu.VMEM(x.shape, BF),
            pltpu.VMEM((4, 8) + w.shape, BF),
            pltpu.VMEM((d, lanes), F32),
            pltpu.VMEM((d, cols), F32),
            pltpu.VMEM((4, IM, 8, d + EXTRA), BF),
            pltpu.VMEM((4, IM, 8, d + EXTRA), BF),
            pltpu.VMEM((IM, 8, d + EXTRA), BF),
            pltpu.VMEM((IM, 8, d + EXTRA), BF),
            pltpu.VMEM((8, IM, d + EXTRA), F32),
            pltpu.VMEM(block, BF),
            pltpu.VMEM((8, NZ * NY, IM, d), BF),
            pltpu.VMEM((8, NZ * NY, IM, d), BF),
            pltpu.VMEM((experts, NZ * NY * IM, f), BF),
            pltpu.VMEM((experts, NZ * NY * IM, f), BF),
            pltpu.VMEM((NZ, NY // 2, 2) + block, BF),
            pltpu.VMEM((NZ,) + block, BF),
            pltpu.VMEM((NZ,) + block, BF),
            pltpu.VMEM(block, F32),
            pltpu.VMEM((IM, 8, d + EXTRA), F32),
            pltpu.VMEM((IM, 8, d + EXTRA), BF),
            pltpu.VMEM((4, IM, 8, d + EXTRA), BF),
            pltpu.VMEM((NE, feats // 2, lanes), BF),
            *two(NE), *two(4), *two(8), *two(IM, 4), *two(IM), *two(NZ), ring, ring,
            *two(NZ), ring, ring, *two(IM, 4), *two(IM), *two(NE),
        ],
        compiler_params=pltpu.CompilerParams(
            collective_id=0, has_side_effects=True, vmem_limit_bytes=48 * 2**20
        ),
    )(x, w, win, wout)


def local(tokens, slot_params, w_in, w_out, out_grad):
    images, patches, feats = tokens.shape
    m = patches // 4
    slots = slot_params.shape[1]

    def cut(x):
        return jnp.transpose(x.reshape(images, 4, m, feats), (0, 1, 3, 2)).reshape(NE, feats, m)

    packed = jnp.concatenate([cut(tokens), cut(out_grad)], 2)
    params = jnp.transpose(slot_params.reshape(feats, IM, 4, 1, 4), (0, 2, 1, 3, 4))
    params = jnp.broadcast_to(params, (feats, 4, IM, 2, 4)).reshape(feats, 2 * slots)
    grad, grad_w_in, grad_w_out = whole(packed, params, jnp.swapaxes(w_in, 1, 2), w_out)
    grad = jnp.transpose(grad.reshape(images, 4, feats // 2, 2, m), (0, 1, 4, 3, 2))
    return (grad.reshape(images, patches, feats), jnp.swapaxes(grad_w_in, 1, 2), grad_w_out)


def solution(mesh):
    return jax.shard_map(
        local,
        mesh=mesh,
        in_specs=(
            P("dp", None, "expert"),
            P("expert", None),
            P("expert", None, "dp"),
            P("expert", "dp", None),
            P("dp", None, "expert"),
        ),
        out_specs=(P("dp", None, "expert"), P("expert", None, "dp"), P("expert", "dp", None)),
        check_vma=False,
    )
```

time: 1460 us -> 156 us (0.11)
  waiting for transfers between devices: 1180 us -> 0 us
  Pallas kernels: 0 us -> 150 us
  blocking collectives: 146 us -> 0 us
  starting transfers between devices: 74.9 us -> 0 us
  matrix products: 16.4 us -> 0 us
  other arithmetic: 16.4 us -> 0.13 us
    psum x2 -> x0, waiting for transfers between devices: 617 us -> none  [the longest x1 347 us: local(): dcomb, ddisp = lax.psum((dcomb, ddisp), 'expert')]
    unnamed x8 -> x0, waiting for transfers between devices: 286 us -> none
    all_gather x2 -> x0, waiting for transfers between devices: 261 us -> none  [the longest x1 153 us: local(): lax.all_gather(grads, 'dp', axis=0, tiled=True)]
    pallas_call x0 -> x1, Pallas kernels: none -> 150 us  [whole(): pl.pallas_call(whole_kernel, out_shape=(jax.ShapeDtypeStruct((NE, feats /...]
    psum x1 -> x0, blocking collectives: 99.7 us -> none  [local(): prod, row_sq, col_sq = lax.psum((prod, row_sq, col_sq), 'expert')]
    all_to_all x2 -> x0, starting transfers between devices: 74.4 us -> none  [the longest x1 37.4 us: local(): lax.all_to_all(summed_out.astype(jnp.bfloat16), 'expert', split_axis=2, c...]
    all_to_all x2 -> x0, blocking collectives: 46.5 us -> none  [the longest x1 28.2 us: local(): lax.all_to_all(slot_in, 'expert', split_axis=1, concat_axis=2, tiled=True)]
    dot_general x13 -> x0, matrix products: 16.4 us -> none  [the longest x1 2.3 us: local(): jnp.einsum('imd,ds->ims', tokens, slot_params, preferred_element_type=jnp...]
  transfers between devices with their start and end apart: 8 -> 0, of which waited for: 7 -> 0; matrix products, arithmetic and copies ran while one was open for 1% -> 0% of each run, Pallas kernels for 0% -> 0%
where the time goes in v2:
time: 156 us
  Pallas kernels  150 us (96%)
  local copies, waits for them, and re-layouts  5.69 us (4%)
    pallas_call x1, Pallas kernels, whole(): pl.pallas_call(whole_kernel, out_shape=(jax.ShapeDtypeStruct((NE, feats /...  150 us
    unnamed x11, local copies, waits for them, and re-layouts  4.21 us

profile of v2, /device:TPU:1, one launch (start us, length us, event | category | flops | bytes accessed | tf_op | source)
XLA Modules:
  0.0 156.2 jit_solution(6646919688483072984)
XLA Ops:
  0.6 0.8 copy.20
  1.5 0.0 copy-start.2
  1.5 0.0 copy-start.3
  1.5 0.1 copy.22.w_ref
  1.6 0.8 copy-done.2
  2.4 0.0 copy-start.1
  2.4 0.1 reshape.30
  2.5 0.0 copy-start
  2.5 0.1 copy.18
  2.6 0.0 copy-done.3
  2.6 0.1 reshape.32
  2.7 0.1 copy.19
  2.8 0.1 pad_maximum_fusion.x_ref
  2.9 0.6 copy-done.1
  3.5 0.3 copy-done
  3.8 149.6 %shard_map.76 = (bf16[32,10,128]{2,1,0:T(8,128)(2,1)S(1)}, bf16[4,160,640]{2,1,0:T(8,128)(2,1)S(1)}, bf16[4,160,640]{2,1,0:T(8,128)(2,1)S(1)}) custom-call(bf16[32,20,128]{2,1,0:T(8,128)(2,1)S(1)} %pad_maximum_fusion.x_ref, bf16[20,256]{1,0:T(8,128)(2,1)S(1)} %copy.22.w_ref, bf16[4,160,640]{2,1,0:T(8,128)(2,1)S(1)} %bitcast.23, ...), custom_call_target="tpu_custom_call" | custom-call | tf_op jit(solution)/shard_map/pallas_call | solution.py:460
  153.4 0.1 reshape.36
  153.6 0.8 reshape.37
  154.4 0.9 copy.27
  155.3 0.9 copy.28
  (4 shorter events, 0.1 us)
Async XLA Ops:
  1.5 0.9 copy-start.2
  1.5 1.1 copy-start.3
  2.4 1.2 copy-start.1
  2.5 1.3 copy-start

commit v3 on v2

--- a/solution.py
+++ b/solution.py
@@ -70,28 +70,37 @@
     others = [at(z, y + 1), at(z, y + NY - 1)] + [at(z + k, y) for k in range(1, NZ)]
     for other in others:
         pl.semaphore_signal(barrier, inc=1, device_id={"dp": other}, device_id_type=MESH)
-    pl.semaphore_wait(barrier, NE - 1 + len(others))
+    return lambda: pl.semaphore_wait(barrier, NE - 1 + len(others))
 
 
 def spread(x_ref, y_ref, sems):
     me = lax.axis_index("expert")
+    hi, lo = lax.div(me, 8), lax.rem(me, 8)
     send_sem, recv_sem = sems
 
-    def copy(k):
-        to = lax.rem(me + k, NE)
-        return send(x_ref.at[to], y_ref.at[me], send_sem.at[k], recv_sem.at[k], expert=to)
-
-    def start(k, carry):
-        copy(k).start()
+    def copy(dz, k):
+        to = lax.rem(hi + dz, 4) * 8 + lax.rem(lo + k, 8)
+        at_sem = dz * 8 + k
+        return send(
+            x_ref.at[to], y_ref.at[me], send_sem.at[at_sem], recv_sem.at[at_sem], expert=to
+        )
+
+    def start(dz, k, carry):
+        copy(dz, k).start()
         return carry
 
-    def finish(k, carry):
-        copy(k).wait()
+    def finish(dz, k, carry):
+        copy(dz, k).wait()
         return carry
 
-    lax.fori_loop(1, NE, start, 0)
+    def finish_all():
+        for dz in (0, 1, 3, 2):
+            lax.fori_loop(0 if dz else 1, 8, functools.partial(finish, dz), 0)
+
+    for dz in (2, 1, 3, 0):
+        lax.fori_loop(0 if dz else 1, 8, functools.partial(start, dz), 0)
     y_ref[me] = x_ref[me]
-    return lambda: lax.fori_loop(1, NE, finish, 0)
+    return finish_all
 
 
 def share_along(w_ref, v_ref, sems):
@@ -121,13 +130,19 @@
     return copies
 
 
+STEPS = ((2, 0), (2, 1), (1, 0), (3, 0), (1, 1), (3, 1), (0, 1), (0, 0))
+
+
+def moved(j, dz, dx):
+    return lax.rem(lax.div(j, 2) + dz, 4) * 2 + lax.rem(j + dx, 2)
+
+
 def collect(x_ref, o_ref, part, total, q_sems, j_sems):
     me = lax.axis_index("expert")
     j, q = lax.div(me, 4), lax.rem(me, 4)
     q_copies, j_copies = {}, {}
-    steps = list(range(1, IM)) + [0]
-    for step in steps:
-        to = lax.rem(j + step, IM)
+    for step, (dz, dx) in enumerate(STEPS):
+        to = moved(j, dz, dx)
         for k in range(1, 4):
             q_copies[step, k] = send(
                 x_ref.at[lax.rem(q + k, 4), to],
@@ -137,14 +152,14 @@
                 expert=team(j, q + k),
             )
             q_copies[step, k].start()
-    for step in steps:
-        to = lax.rem(j + step, IM)
+    for step, (dz, dx) in enumerate(STEPS):
+        to = moved(j, dz, dx)
         for k in range(1, 4):
             q_copies[step, k].wait_recv()
         summed = x_ref[q, to].astype(F32)
         for k in range(1, 4):
             summed = summed + part[k, step].astype(F32)
-        if step == 0:
+        if (dz, dx) == (0, 0):
             o_ref[j] = summed.astype(BF)
             continue
         total[step] = summed.astype(BF)
@@ -166,8 +181,8 @@
     me = lax.axis_index("expert")
     j, q = lax.div(me, 4), lax.rem(me, 4)
     q_copies, j_copies = {}, {}
-    for step in range(1, IM):
-        to = lax.rem(j + step, IM)
+    for step, (dz, dx) in enumerate(STEPS[:-1]):
+        to = moved(j, dz, dx)
         j_copies[step] = send(
             x_ref.at[to],
             o_ref.at[q, j],
@@ -177,9 +192,10 @@
         )
         j_copies[step].start()
     o_ref[q, j] = x_ref[j]
-    for step in range(IM):
-        here = lax.rem(j + IM - step, IM)
-        if step:
+    for step in range(IM - 1, -1, -1):
+        dz, dx = STEPS[step]
+        here = moved(j, 4 - dz, dx)
+        if step in j_copies:
             j_copies[step].wait_recv()
         for k in range(1, 4):
             q_copies[step, k] = send(
@@ -196,13 +212,22 @@
         copy.wait_send()
 
 
-def gather(b_ref, y_ref, z, y, z_sems, y_sems):
+ZF = 6
+HALF = NY // 2
+
+
+def ring_rows(step, way, first, count):
+    if step < HALF:
+        return pl.ds(first, count)
+    return pl.ds(first + way * (count // 2), count // 2)
+
+
+def gather(b_ref, y_ref, z, y, z_sems, y_sems, zb_sems, yb_sems):
     p = at(z, y)
 
     def y_copy(chain, step, way):
-        back = NY - (step - 1) if way == 0 else step - 1
-        slot = at(z + chain, y + back)
-        rows = pl.ds(0, 8) if step < NY // 2 else pl.ds(4 * way, 4)
+        slot = at(z + chain, y + (NY - (step - 1) if way == 0 else step - 1))
+        rows = ring_rows(step, way, 0, ZF)
         src = b_ref if chain == 0 and step == 1 else y_ref.at[:, slot]
         return send(
             src.at[rows],
@@ -212,43 +237,116 @@
             dp=at(z, y + (1 if way == 0 else NY - 1)),
         )
 
-    y_copies, z_copies = {}, {}
-    for way in (0, 1):
-        y_copies[0, 1, way] = y_copy(0, 1, way)
-        y_copies[0, 1, way].start()
+    def yb_copy(step, way):
+        slot = at(z, y + (NY - (step - 1) if way == 0 else step - 1))
+        rows = ring_rows(step, way, ZF, 8 - ZF)
+        src = b_ref if step == 1 else y_ref.at[:, slot]
+        return send(
+            src.at[rows],
+            y_ref.at[rows, slot],
+            yb_sems[0].at[step, way],
+            yb_sems[1].at[step, way],
+            dp=at(z, y + (1 if way == 0 else NY - 1)),
+        )
+
+    def zb_copy(dy, k):
+        rows = pl.ds(ZF, 8 - ZF)
+        slot = at(z, y + dy)
+        src = b_ref if dy == 0 else y_ref.at[:, slot]
+        return send(
+            src.at[rows],
+            y_ref.at[rows, slot],
+            zb_sems[0].at[dy, k],
+            zb_sems[1].at[dy, k],
+            dp=at(z + k, y),
+        )
+
+    y_copies, z_copies, yb_copies, zb_copies = {}, {}, {}, {}
+
+    def ring(chain, step):
+        if step > 1:
+            for way in (0, 1):
+                y_copies[chain, step - 1, way].wait_recv()
+        elif chain:
+            z_copies[NZ - chain].wait_recv()
+        for way in (0, 1):
+            y_copies[chain, step, way] = y_copy(chain, step, way)
+            y_copies[chain, step, way].start()
+
+    def fan(dy):
+        for k in (1, 3, 2):
+            zb_copies[dy, k] = zb_copy(dy, k)
+            zb_copies[dy, k].start()
+
+    def ring_b(step):
+        if step > 1:
+            for way in (0, 1):
+                yb_copies[step - 1, way].wait_recv()
+        if step <= HALF:
+            for way in (0, 1):
+                yb_copies[step, way] = yb_copy(step, way)
+                yb_copies[step, way].start()
+        if 1 < step <= HALF:
+            fan(step - 1)
+            fan(NY - (step - 1))
+        elif step > HALF:
+            fan(HALF)
+
+    ring_b(1)
+    ring(0, 1)
     for k in (3, 1, 2):
         z_copies[k] = send(
-            b_ref, y_ref.at[:, p], z_sems[0].at[k], z_sems[1].at[k], dp=at(z + k, y)
+            b_ref.at[pl.ds(0, ZF)],
+            y_ref.at[pl.ds(0, ZF), p],
+            z_sems[0].at[k],
+            z_sems[1].at[k],
+            dp=at(z + k, y),
         )
         z_copies[k].start()
+    fan(0)
     y_ref[:, p] = b_ref[...]
-    for chain in (1, 3, 2):
-        z_copies[NZ - chain].wait_recv()
-        for way in (0, 1):
-            y_copies[chain, 1, way] = y_copy(chain, 1, way)
-            y_copies[chain, 1, way].start()
-    for step in range(2, NY // 2 + 1):
-        for chain in (0, 1, 3, 2):
-            for way in (0, 1):
-                y_copies[chain, step - 1, way].wait_recv()
-                y_copies[chain, step, way] = y_copy(chain, step, way)
-                y_copies[chain, step, way].start()
+    ring_b(2)
+    ring(0, 2)
+    ring(1, 1)
+    ring(3, 1)
+    ring_b(3)
+    ring(0, 3)
+    ring(2, 1)
+    ring(1, 2)
+    ring(3, 2)
+    ring_b(4)
+    ring(0, 4)
+    ring(2, 2)
+    ring(1, 3)
+    ring(3, 3)
+    ring_b(5)
+    ring(2, 3)
+    ring(1, 4)
+    ring(3, 4)
+    ring(2, 4)
     for chain in (0, 1, 3, 2):
         for way in (0, 1):
-            y_copies[chain, NY // 2, way].wait_recv()
-    for copy in z_copies.values():
-        copy.wait_send()
-    for copy in y_copies.values():
-        copy.wait_send()
-
-
-def scatter(p_ref, total, ring, z_out, z_in, z, y, z_sems, y_sems, meanwhile):
-    half = NY // 2
+            y_copies[chain, HALF, way].wait_recv()
+    for copy in zb_copies.values():
+        copy.wait()
+    for copies in (z_copies, y_copies, yb_copies):
+        for copy in copies.values():
+            copy.wait_send()
+
+
+def scatter(
+    p_ref, total, ring, z_out, z_in, ring_b, zb_in,
+    z, y, z_sems, y_sems, zb_sems, yb_sems, meanwhile,
+):
+    last = 8 - ZF
+
+    def ahead(step, way):
+        return step if way == 0 else NY - step
 
     def y_copy(chain, step, way):
-        slot = at(z + chain, y + (step if way == 0 else NY - step))
-        rows = pl.ds(4 * way, 4) if step == half else pl.ds(0, 8)
-        src = p_ref.at[:, slot] if step == half else ring.at[chain, step, way]
+        slot = at(z + chain, y + ahead(step, way))
+        rows = ring_rows(step, way, 0, ZF)
+        src = p_ref.at[:, slot] if step == HALF else ring.at[chain, step, way]
         return send(
             src.at[rows],
             ring.at[chain, step - 1, way, rows],
@@ -257,30 +355,78 @@
             dp=at(z, y + (1 if way == 0 else NY - 1)),
         )
 
+    def yb_copy(step, way):
+        rows = ring_rows(step, way, 0, last)
+        return send(
+            ring_b.at[step, way, rows],
+            ring_b.at[step - 1, way, rows],
+            yb_sems[0].at[step, way],
+            yb_sems[1].at[step, way],
+            dp=at(z, y + (1 if way == 0 else NY - 1)),
+        )
+
     order = (1, 3, 2, 0)
-    y_copies, z_copies = {}, {}
+    y_copies, z_copies, yb_copies, zb_copies = {}, {}, {}, {}
     for chain in order:
         for way in (0, 1):
-            y_copies[chain, half, way] = y_copy(chain, half, way)
-            y_copies[chain, half, way].start()
+            y_copies[chain, HALF, way] = y_copy(chain, HALF, way)
+            y_copies[chain, HALF, way].start()
+    for dy in (4, 3, 5, 2, 6, 1, 7, 0):
+        for k in (2, 1, 3):
+            zb_copies[dy, k] = send(
+                p_ref.at[pl.ds(ZF, last), at(z + k, y + dy)],
+                zb_in.at[dy, k],
+                zb_sems[0].at[dy, k],
+                zb_sems[1].at[dy, k],
+                dp=at(z + k, y),
+            )
+            zb_copies[dy, k].start()
     meanwhile()
-    for step in range(half - 1, 0, -1):
+
+    def along_z(dy, a):
+        here = p_ref[ZF + a, at(z, y + dy)].astype(F32)
+        for k in (1, 2, 3):
+            here = here + zb_in[dy, k, a].astype(F32)
+        return here
+
+    def step_b(step):
+        for way in (0, 1):
+            dy = ahead(step, way)
+            if step < HALF:
+                yb_copies[step + 1, way].wait_recv()
+            if step < HALF or way == 0:
+                for k in (1, 2, 3):
+                    zb_copies[dy, k].wait_recv()
+            for a in range(last):
+                half = a // (last // 2) == way
+                if step == HALF and not half:
+                    continue
+                mine = along_z(dy, a)
+                if step < HALF - 1 or (step == HALF - 1 and half):
+                    mine = mine + ring_b[step, way, a].astype(F32)
+                ring_b[step, way, a] = mine.astype(BF)
+            yb_copies[step, way] = yb_copy(step, way)
+            yb_copies[step, way].start()
+
+    step_b(HALF)
+    for step in range(HALF - 1, 0, -1):
         for chain in order:
             for way in (0, 1):
                 y_copies[chain, step + 1, way].wait_recv()
-                slot = at(z + chain, y + (step if way == 0 else NY - step))
-                for a in range(8):
+                slot = at(z + chain, y + ahead(step, way))
+                for a in range(ZF):
                     mine = p_ref[a, slot]
-                    if step < half - 1 or a // 4 == way:
+                    if step < HALF - 1 or a // (ZF // 2) == way:
                         mine = (mine.astype(F32) + ring[chain, step, way, a].astype(F32)).astype(BF)
                     ring[chain, step, way, a] = mine
                 y_copies[chain, step, way] = y_copy(chain, step, way)
                 y_copies[chain, step, way].start()
+        step_b(step)
     for chain in order:
         for way in (0, 1):
             y_copies[chain, 1, way].wait_recv()
         here = at(z + chain, y)
-        for a in range(8):
+        for a in range(ZF):
             summed = (
                 p_ref[a, here].astype(F32)
                 + ring[chain, 0, 0, a].astype(F32)
@@ -299,42 +445,78 @@
                 dp=at(z + chain, y),
             )
             z_copies[chain].start()
+    for way in (0, 1):
+        yb_copies[1, way].wait_recv()
+    for k in (1, 2, 3):
+        zb_copies[0, k].wait_recv()
+    for a in range(last):
+        total[ZF + a] = (
+            along_z(0, a) + ring_b[0, 0, a].astype(F32) + ring_b[0, 1, a].astype(F32)
+        )
     for chain in (1, 3, 2):
         z_copies[chain].wait_recv()
-    for a in range(8):
+    for a in range(ZF):
         total[a] = (
             total[a]
             + z_in[1, a].astype(F32)
             + z_in[2, a].astype(F32)
             + z_in[3, a].astype(F32)
         )
-    for copy in z_copies.values():
-        copy.wait_send()
-    for copy in y_copies.values():
-        copy.wait_send()
+    for copies in (z_copies, y_copies, yb_copies, zb_copies):
+        for copy in copies.values():
+            copy.wait_send()
 
 
 def whole_kernel(
-    x_ref, w_ref, win_ref, wout_ref,
+    t_hbm, g_hbm, w_hbm, win_hbm, wout_hbm,
     y_ref, gin_ref, gout_ref,
+    t_ref, g_ref, w_ref, wide, wide_g, x_in, w_in, win_ref, wout_ref, y_in,
     xin, vin, xs, ps, parts, part, part_sum, sums, blk, blkb, every, outs, act_s, dhid_s,
-    ring, z_out, z_in, total, res, resb, back, chunk,
-    s1a, s1b, sa1, sa2, sb1, sb2, cq1, cq2, cj1, cj2, gz1, gz2, gy1, gy2,
-    sz1, sz2, sy1, sy2, bq1, bq2, bj1, bj2, s2a, s2b,
+    ring, z_out, z_in, ring_b, zb_in, total, res, resb, back, chunk,
+    wsem, s1a, s1b, sa1, sa2, sb1, sb2, cq1, cq2, cj1, cj2, gz1, gz2, gy1, gy2, gzb1, gzb2, gyb1, gyb2,
+    sz1, sz2, sy1, sy2, szb1, szb2, syb1, syb2, bq1, bq2, bj1, bj2, s2a, s2b,
 ):
     me = lax.axis_index("expert")
     quarter = lax.rem(me, 4)
     p = lax.axis_index("dp")
     z, y = lax.div(p, NY), lax.rem(p, NY)
-    greet(me, z, y)
-
-    along = share_along(w_ref, vin, (sa1, sa2))
-    finish = spread(x_ref, xin, (s1a, s1b))
+    all_here = greet(me, z, y)
+    pairs = (
+        (t_hbm, t_ref), (g_hbm, g_ref), (w_hbm, w_ref), (win_hbm, win_ref), (wout_hbm, wout_ref)
+    )
+    loads = [
+        pltpu.make_async_copy(src, dst, wsem.at[i]) for i, (src, dst) in enumerate(pairs)
+    ]
+    for load in loads:
+        load.start()
+    for load in loads[:3]:
+        load.wait()
+
+    feats = t_ref.shape[0]
+    for h in (0, 1):
+        lanes = slice(128 * h, 128 * h + 128)
+        wide[h] = t_ref[:, :, lanes].astype(F32).reshape(wide.shape[1:])
+        wide_g[h] = g_ref[:, :, lanes].astype(F32).reshape(wide.shape[1:])
+    left = lax.broadcasted_iota(jnp.int32, (1, 128), 1) < 64
+    for j in range(IM):
+        for h in (0, 1):
+            t = wide[h, pl.ds(j, feats, IM), :]
+            g = wide_g[h, pl.ds(j, feats, IM), :]
+            x_in[4 * j + 2 * h] = jnp.where(left, t, pltpu.roll(g, 64, 1)).astype(BF)
+            x_in[4 * j + 2 * h + 1] = jnp.where(left, pltpu.roll(t, 64, 1), g).astype(BF)
+    slots = w_ref.shape[1]
+    col = lax.broadcasted_iota(jnp.int32, (slots, 2 * slots), 1)
+    slot = ((col >> 3) & 7) * 16 + (col >> 6) * 4 + (col & 3)
+    pick = lax.broadcasted_iota(jnp.int32, (slots, 2 * slots), 0) == slot
+    w_in[...] = mm(w_ref[...], jnp.where(pick, 1.0, 0.0).astype(BF)).astype(BF)
+    all_here()
+
+    along = share_along(w_in, vin, (sa1, sa2))
+    finish = spread(x_in, xin, (s1a, s1b))
     for copy in along:
         copy.wait()
     across = share_across(vin, (sb1, sb2))
     finish()
-    feats = xin.shape[1]
     for e in range(NE):
         xs[e * feats : (e + 1) * feats, :] = xin[e].astype(F32)
     both = xs[...].T
@@ -372,13 +554,15 @@
         val = sums[j, :, :D].astype(F32)
         den = jnp.sum(sums[j, :, D:].astype(F32), 1, keepdims=True)
         val = val * jnp.where(top, 1.0 / den, 1.0)
-        wide = jnp.broadcast_to(den, (8, EXTRA))
+        den_wide = jnp.broadcast_to(den, (8, EXTRA))
         for a in range(8):
             blk[a, j : j + 1, :D] = val[a : a + 1]
-            blk[a, j : j + 1, D:] = wide[a : a + 1]
+            blk[a, j : j + 1, D:] = den_wide[a : a + 1]
     for a in range(8):
         blkb[a] = blk[a, :, :D].astype(BF)
-    gather(blkb, every, z, y, (gz1, gz2), (gy1, gy2))
+    gather(blkb, every, z, y, (gz1, gz2), (gy1, gy2), (gzb1, gzb2), (gyb1, gyb2))
+    for load in loads[3:]:
+        load.wait()
 
     rows = NZ * NY * IM
 
@@ -404,7 +588,8 @@
 
     lax.fori_loop(0, 4, forward, 0)
     scatter(
-        outs, total, ring, z_out, z_in, z, y, (sz1, sz2), (sy1, sy2),
+        outs, total, ring, z_out, z_in, ring_b, zb_in, z, y,
+        (sz1, sz2), (sy1, sy2), (szb1, szb2), (syb1, syb2),
         lambda: lax.fori_loop(0, 4, weight_grads, 0),
     )
 
@@ -443,32 +628,57 @@
     for e in range(NE):
         a, b, c = e * feats, e * feats + feats // 2, (e + 1) * feats
         chunk[e] = jnp.where(low, xs[a:b, :], xs[b:c, :]).astype(BF)
-    spread(chunk, y_ref, (s2a, s2b))()
-
-
-def whole(x, w, win, wout):
-    _, feats, lanes = x.shape
-    cols = w.shape[1]
+    spread(chunk, y_in, (s2a, s2b))()
+    for j in range(IM):
+        for h in (0, 1):
+            a, b = y_in[4 * j + 2 * h].astype(F32), y_in[4 * j + 2 * h + 1].astype(F32)
+            wide[h, pl.ds(j, feats // 2, IM), :] = jnp.where(left, a, pltpu.roll(b, 64, 1))
+            wide[h, pl.ds(IM * (feats // 2) + j, feats // 2, IM), :] = jnp.where(
+                left, pltpu.roll(a, 64, 1), b
+            )
+    for h in (0, 1):
+        lanes = slice(128 * h, 128 * h + 128)
+        y_ref[:, :, lanes] = wide[h].reshape(feats, IM, 128).astype(BF)
+
+
+def whole(t, g, w, win, wout):
+    feats, _, patches = t.shape
+    lanes = patches // 2
+    slots = w.shape[1]
+    cols = 2 * slots
     experts, f, d = win.shape
     dma = pltpu.SemaphoreType.DMA
-    ring = dma((NZ, NY // 2 + 1, 2))
+    ring = dma((NZ, HALF + 1, 2))
+    last = 8 - ZF
 
     def two(*shape):
         return [dma(shape), dma(shape)]
 
     block = (8, IM, d)
+    vmem = pl.BlockSpec(memory_space=pltpu.VMEM)
+    hbm = pl.BlockSpec(memory_space=pl.ANY)
     return pl.pallas_call(
         whole_kernel,
         out_shape=(
-            jax.ShapeDtypeStruct((NE, feats // 2, lanes), BF),
+            jax.ShapeDtypeStruct(t.shape, BF),
             jax.ShapeDtypeStruct(win.shape, BF),
             jax.ShapeDtypeStruct(win.shape, BF),
         ),
-        in_specs=[pl.BlockSpec(memory_space=pltpu.VMEM)] * 4,
-        out_specs=(pl.BlockSpec(memory_space=pltpu.VMEM),) * 3,
+        in_specs=[hbm] * 5,
+        out_specs=(vmem,) * 3,
         scratch_shapes=[
-            pltpu.VMEM(x.shape, BF),
-            pltpu.VMEM((4, 8) + w.shape, BF),
+            pltpu.VMEM(t.shape, BF),
+            pltpu.VMEM(t.shape, BF),
+            pltpu.VMEM(w.shape, BF),
+            pltpu.VMEM((2, feats * IM, lanes), F32),
+            pltpu.VMEM((2, feats * IM, lanes), F32),
+            pltpu.VMEM((NE, feats, lanes), BF),
+            pltpu.VMEM((feats, cols), BF),
+            pltpu.VMEM(win.shape, BF),
+            pltpu.VMEM(win.shape, BF),
+            pltpu.VMEM((NE, feats // 2, lanes), BF),
+            pltpu.VMEM((NE, feats, lanes), BF),
+            pltpu.VMEM((4, 8, feats, cols), BF),
             pltpu.VMEM((d, lanes), F32),
             pltpu.VMEM((d, cols), F32),
             pltpu.VMEM((4, IM, 8, d + EXTRA), BF),
@@ -481,37 +691,36 @@
             pltpu.VMEM((8, NZ * NY, IM, d), BF),
             pltpu.VMEM((experts, NZ * NY * IM, f), BF),
             pltpu.VMEM((experts, NZ * NY * IM, f), BF),
-            pltpu.VMEM((NZ, NY // 2, 2) + block, BF),
-            pltpu.VMEM((NZ,) + block, BF),
-            pltpu.VMEM((NZ,) + block, BF),
+            pltpu.VMEM((NZ, HALF, 2, ZF, IM, d), BF),
+            pltpu.VMEM((NZ, ZF, IM, d), BF),
+            pltpu.VMEM((NZ, ZF, IM, d), BF),
+            pltpu.VMEM((HALF + 1, 2, last, IM, d), BF),
+            pltpu.VMEM((NY, NZ, last, IM, d), BF),
             pltpu.VMEM(block, F32),
             pltpu.VMEM((IM, 8, d + EXTRA), F32),
             pltpu.VMEM((IM, 8, d + EXTRA), BF),
             pltpu.VMEM((4, IM, 8, d + EXTRA), BF),
             pltpu.VMEM((NE, feats // 2, lanes), BF),
-            *two(NE), *two(4), *two(8), *two(IM, 4), *two(IM), *two(NZ), ring, ring,
-            *two(NZ), ring, ring, *two(IM, 4), *two(IM), *two(NE),
+            dma((5,)), *two(NE), *two(4), *two(8), *two(IM, 4), *two(IM),
+            *two(NZ), ring, ring, *two(NY, NZ), *two(HALF + 1, 2),
+            *two(NZ), ring, ring, *two(NY, NZ), *two(HALF + 1, 2),
+            *two(IM, 4), *two(IM), *two(NE),
         ],
         compiler_params=pltpu.CompilerParams(
-            collective_id=0, has_side_effects=True, vmem_limit_bytes=48 * 2**20
+            collective_id=0, has_side_effects=True, vmem_limit_bytes=52 * 2**20
         ),
-    )(x, w, win, wout)
+    )(t, g, w, win, wout)
 
 
 def local(tokens, slot_params, w_in, w_out, out_grad):
-    images, patches, feats = tokens.shape
-    m = patches // 4
-    slots = slot_params.shape[1]
-
-    def cut(x):
-        return jnp.transpose(x.reshape(images, 4, m, feats), (0, 1, 3, 2)).reshape(NE, feats, m)
-
-    packed = jnp.concatenate([cut(tokens), cut(out_grad)], 2)
-    params = jnp.transpose(slot_params.reshape(feats, IM, 4, 1, 4), (0, 2, 1, 3, 4))
-    params = jnp.broadcast_to(params, (feats, 4, IM, 2, 4)).reshape(feats, 2 * slots)
-    grad, grad_w_in, grad_w_out = whole(packed, params, jnp.swapaxes(w_in, 1, 2), w_out)
-    grad = jnp.transpose(grad.reshape(images, 4, feats // 2, 2, m), (0, 1, 4, 3, 2))
-    return (grad.reshape(images, patches, feats), jnp.swapaxes(grad_w_in, 1, 2), grad_w_out)
+    grad, grad_w_in, grad_w_out = whole(
+        jnp.transpose(tokens, (2, 0, 1)),
+        jnp.transpose(out_grad, (2, 0, 1)),
+        slot_params,
+        jnp.swapaxes(w_in, 1, 2),
+        w_out,
+    )
+    return (jnp.transpose(grad, (1, 2, 0)), jnp.swapaxes(grad_w_in, 1, 2), grad_w_out)
 
 
 def solution(mesh):

time: 156 us -> 148 us (0.949)
  Pallas kernels: 150 us -> 143 us
    pallas_call x1, Pallas kernels: 150 us -> 143 us  [whole(): pl.pallas_call(whole_kernel, out_shape=(jax.ShapeDtypeStruct(t.shape, BF)...]
    unnamed x11 -> x9, local copies, waits for them, and re-layouts: 4.21 us -> 4.88 us
where the time goes in v3:
time: 148 us
  Pallas kernels  143 us (97%)
  local copies, waits for them, and re-layouts  4.88 us (3%)
    pallas_call x1, Pallas kernels, whole(): pl.pallas_call(whole_kernel, out_shape=(jax.ShapeDtypeStruct(t.shape, BF)...  143 us
    unnamed x9, local copies, waits for them, and re-layouts  4.88 us

profile of v3, /device:TPU:1, one launch (start us, length us, event | category | flops | bytes accessed | tf_op | source)
XLA Modules:
  0.0 148.1 jit_solution(16550248807214608205)
XLA Ops:
  0.6 0.0 copy-start
  0.6 0.9 copy-done
  1.5 0.0 copy-start.1
  1.5 0.9 copy-done.1
  2.4 0.0 copy-start.2
  2.4 0.7 copy-done.2
  3.1 142.5 %shard_map.76 = (bf16[20,8,256]{2,1,0:T(8,128)(2,1)S(1)}, bf16[4,160,640]{2,1,0:T(8,128)(2,1)S(1)}, bf16[4,160,640]{2,1,0:T(8,128)(2,1)S(1)}) custom-call(bf16[20,8,256]{2,1,0:T(8,128)(2,1)S(1)} %bitcast.6, bf16[20,8,256]{2,1,0:T(8,128)(2,1)S(1)} %bitcast.7, bf16[20,128]{1,0:T(8,128)(2,1)S(1)} %copy-done.2, bf16[4,160,640]{2,1,0:T(8,128)(2,1)} %bitcast.9, ...), custom_call_target="tpu_custom_call" | custom-call | tf_op jit(solution)/shard_map/pallas_call | solution.py:660
  145.6 0.6 copy.11
  146.3 0.9 copy.12
  147.2 0.9 copy.13
Async XLA Ops:
  0.6 0.9 copy-start
  1.5 0.9 copy-start.1
  2.4 0.7 copy-start.2

commit v4 on v3

--- a/solution.py
+++ b/solution.py
@@ -286,11 +286,6 @@
             for way in (0, 1):
                 yb_copies[step, way] = yb_copy(step, way)
                 yb_copies[step, way].start()
-        if 1 < step <= HALF:
-            fan(step - 1)
-            fan(NY - (step - 1))
-        elif step > HALF:
-            fan(HALF)
 
     ring_b(1)
     ring(0, 1)
@@ -303,23 +298,30 @@
             dp=at(z + k, y),
         )
         z_copies[k].start()
-    fan(0)
     y_ref[:, p] = b_ref[...]
     ring_b(2)
     ring(0, 2)
     ring(1, 1)
     ring(3, 1)
+    fan(0)
     ring_b(3)
     ring(0, 3)
     ring(2, 1)
+    fan(1)
+    fan(7)
     ring(1, 2)
     ring(3, 2)
     ring_b(4)
+    fan(2)
+    fan(6)
     ring(0, 4)
     ring(2, 2)
     ring(1, 3)
     ring(3, 3)
     ring_b(5)
+    fan(3)
+    fan(5)
+    fan(4)
     ring(2, 3)
     ring(1, 4)
     ring(3, 4)
@@ -336,7 +338,7 @@
 
 def scatter(
     p_ref, total, ring, z_out, z_in, ring_b, zb_in,
-    z, y, z_sems, y_sems, zb_sems, yb_sems, meanwhile,
+    z, y, z_sems, y_sems, zb_sems, yb_sems,
 ):
     last = 8 - ZF
 
@@ -381,7 +383,6 @@
                 dp=at(z + k, y),
             )
             zb_copies[dy, k].start()
-    meanwhile()
 
     def along_z(dy, a):
         here = p_ref[ZF + a, at(z, y + dy)].astype(F32)
@@ -468,9 +469,9 @@
 
 
 def whole_kernel(
-    t_hbm, g_hbm, w_hbm, win_hbm, wout_hbm,
+    tgw_ref, win_hbm, wout_hbm,
     y_ref, gin_ref, gout_ref,
-    t_ref, g_ref, w_ref, wide, wide_g, x_in, w_in, win_ref, wout_ref, y_in,
+    wide, wide_g, wide_w, x_in, w_in, win_ref, wout_ref, y_in,
     xin, vin, xs, ps, parts, part, part_sum, sums, blk, blkb, every, outs, act_s, dhid_s,
     ring, z_out, z_in, ring_b, zb_in, total, res, resb, back, chunk,
     wsem, s1a, s1b, sa1, sa2, sb1, sb2, cq1, cq2, cj1, cj2, gz1, gz2, gy1, gy2, gzb1, gzb2, gyb1, gyb2,
@@ -481,22 +482,18 @@
     p = lax.axis_index("dp")
     z, y = lax.div(p, NY), lax.rem(p, NY)
     all_here = greet(me, z, y)
-    pairs = (
-        (t_hbm, t_ref), (g_hbm, g_ref), (w_hbm, w_ref), (win_hbm, win_ref), (wout_hbm, wout_ref)
-    )
+    pairs = ((win_hbm, win_ref), (wout_hbm, wout_ref))
     loads = [
         pltpu.make_async_copy(src, dst, wsem.at[i]) for i, (src, dst) in enumerate(pairs)
     ]
     for load in loads:
         load.start()
-    for load in loads[:3]:
-        load.wait()
-
-    feats = t_ref.shape[0]
+
+    feats = tgw_ref.shape[0]
     for h in (0, 1):
         lanes = slice(128 * h, 128 * h + 128)
-        wide[h] = t_ref[:, :, lanes].astype(F32).reshape(wide.shape[1:])
-        wide_g[h] = g_ref[:, :, lanes].astype(F32).reshape(wide.shape[1:])
+        wide[h] = tgw_ref[:, :IM, lanes].astype(F32).reshape(wide.shape[1:])
+        wide_g[h] = tgw_ref[:, IM : 2 * IM, lanes].astype(F32).reshape(wide.shape[1:])
     left = lax.broadcasted_iota(jnp.int32, (1, 128), 1) < 64
     for j in range(IM):
         for h in (0, 1):
@@ -504,11 +501,13 @@
             g = wide_g[h, pl.ds(j, feats, IM), :]
             x_in[4 * j + 2 * h] = jnp.where(left, t, pltpu.roll(g, 64, 1)).astype(BF)
             x_in[4 * j + 2 * h + 1] = jnp.where(left, pltpu.roll(t, 64, 1), g).astype(BF)
-    slots = w_ref.shape[1]
+    slots = 128
+    wide_w[...] = tgw_ref[:, 2 * IM :, :slots].astype(F32).reshape(wide_w.shape)
+    w = wide_w[pl.ds(0, feats, IM), :].astype(BF)
     col = lax.broadcasted_iota(jnp.int32, (slots, 2 * slots), 1)
     slot = ((col >> 3) & 7) * 16 + (col >> 6) * 4 + (col & 3)
     pick = lax.broadcasted_iota(jnp.int32, (slots, 2 * slots), 0) == slot
-    w_in[...] = mm(w_ref[...], jnp.where(pick, 1.0, 0.0).astype(BF)).astype(BF)
+    w_in[...] = mm(w, jnp.where(pick, 1.0, 0.0).astype(BF)).astype(BF)
     all_here()
 
     along = share_along(w_in, vin, (sa1, sa2))
@@ -561,7 +560,7 @@
     for a in range(8):
         blkb[a] = blk[a, :, :D].astype(BF)
     gather(blkb, every, z, y, (gz1, gz2), (gy1, gy2), (gzb1, gzb2), (gyb1, gyb2))
-    for load in loads[3:]:
+    for load in loads:
         load.wait()
 
     rows = NZ * NY * IM
@@ -590,7 +589,6 @@
     scatter(
         outs, total, ring, z_out, z_in, ring_b, zb_in, z, y,
         (sz1, sz2), (sy1, sy2), (szb1, szb2), (syb1, syb2),
-        lambda: lax.fori_loop(0, 4, weight_grads, 0),
     )
 
     lane = lax.broadcasted_iota(jnp.int32, (8, EXTRA), 1)
@@ -628,7 +626,9 @@
     for e in range(NE):
         a, b, c = e * feats, e * feats + feats // 2, (e + 1) * feats
         chunk[e] = jnp.where(low, xs[a:b, :], xs[b:c, :]).astype(BF)
-    spread(chunk, y_in, (s2a, s2b))()
+    finish = spread(chunk, y_in, (s2a, s2b))
+    lax.fori_loop(0, 4, weight_grads, 0)
+    finish()
     for j in range(IM):
         for h in (0, 1):
             a, b = y_in[4 * j + 2 * h].astype(F32), y_in[4 * j + 2 * h + 1].astype(F32)
@@ -641,10 +641,10 @@
         y_ref[:, :, lanes] = wide[h].reshape(feats, IM, 128).astype(BF)
 
 
-def whole(t, g, w, win, wout):
-    feats, _, patches = t.shape
+def whole(tgw, win, wout):
+    feats, _, patches = tgw.shape
     lanes = patches // 2
-    slots = w.shape[1]
+    slots = 4 * NE
     cols = 2 * slots
     experts, f, d = win.shape
     dma = pltpu.SemaphoreType.DMA
@@ -660,18 +660,16 @@
     return pl.pallas_call(
         whole_kernel,
         out_shape=(
-            jax.ShapeDtypeStruct(t.shape, BF),
+            jax.ShapeDtypeStruct((feats, IM, patches), BF),
             jax.ShapeDtypeStruct(win.shape, BF),
             jax.ShapeDtypeStruct(win.shape, BF),
         ),
-        in_specs=[hbm] * 5,
+        in_specs=[vmem, hbm, hbm],
         out_specs=(vmem,) * 3,
         scratch_shapes=[
-            pltpu.VMEM(t.shape, BF),
-            pltpu.VMEM(t.shape, BF),
-            pltpu.VMEM(w.shape, BF),
             pltpu.VMEM((2, feats * IM, lanes), F32),
             pltpu.VMEM((2, feats * IM, lanes), F32),
+            pltpu.VMEM((feats * IM, lanes), F32),
             pltpu.VMEM((NE, feats, lanes), BF),
             pltpu.VMEM((feats, cols), BF),
             pltpu.VMEM(win.shape, BF),
@@ -701,7 +699,7 @@
             pltpu.VMEM((IM, 8, d + EXTRA), BF),
             pltpu.VMEM((4, IM, 8, d + EXTRA), BF),
             pltpu.VMEM((NE, feats // 2, lanes), BF),
-            dma((5,)), *two(NE), *two(4), *two(8), *two(IM, 4), *two(IM),
+            dma((2,)), *two(NE), *two(4), *two(8), *two(IM, 4), *two(IM),
             *two(NZ), ring, ring, *two(NY, NZ), *two(HALF + 1, 2),
             *two(NZ), ring, ring, *two(NY, NZ), *two(HALF + 1, 2),
             *two(IM, 4), *two(IM), *two(NE),
@@ -709,14 +707,17 @@
         compiler_params=pltpu.CompilerParams(
             collective_id=0, has_side_effects=True, vmem_limit_bytes=52 * 2**20
         ),
-    )(t, g, w, win, wout)
+    )(tgw, win, wout)
 
 
 def local(tokens, slot_params, w_in, w_out, out_grad):
+    images, patches, feats = tokens.shape
+    params = jnp.pad(slot_params, [(0, 0), (0, patches - slot_params.shape[1])])
+    params = jnp.broadcast_to(params[:, None, :], (feats, images, patches))
     grad, grad_w_in, grad_w_out = whole(
-        jnp.transpose(tokens, (2, 0, 1)),
-        jnp.transpose(out_grad, (2, 0, 1)),
-        slot_params,
+        jnp.concatenate(
+            [jnp.transpose(tokens, (2, 0, 1)), jnp.transpose(out_grad, (2, 0, 1)), params], 1
+        ),
         jnp.swapaxes(w_in, 1, 2),
         w_out,
     )

time: 148 us -> 148 us (level)
  local copies, waits for them, and re-layouts: 4.88 us -> 3.29 us
    unnamed x9 -> x5, local copies, waits for them, and re-layouts: 4.88 us -> 2.55 us
where the time goes in v4:
time: 148 us; the launch traced here: 147 us
  Pallas kernels  143 us (97%)
  local copies, waits for them, and re-layouts  3.29 us (2%)
    pallas_call x1, Pallas kernels, whole(): pl.pallas_call(whole_kernel, out_shape=(jax.ShapeDtypeStruct((feats, IM,...  143 us

profile of v4, /device:TPU:1, one launch (start us, length us, event | category | flops | bytes accessed | tf_op | source)
XLA Modules:
  0.0 147.4 jit_solution(11948718731581657580)
XLA Ops:
  0.6 0.0 copy-start
  0.6 0.7 pad.4
  1.4 0.1 copy-done
  1.5 0.9 pad_maximum_fusion.tgw_ref
  2.4 142.5 %shard_map.76 = (bf16[20,8,256]{2,1,0:T(8,128)(2,1)S(1)}, bf16[4,160,640]{2,1,0:T(8,128)(2,1)S(1)}, bf16[4,160,640]{2,1,0:T(8,128)(2,1)S(1)}) custom-call(bf16[20,24,256]{2,1,0:T(8,128)(2,1)S(1)} %pad_maximum_fusion.tgw_ref, bf16[4,160,640]{2,1,0:T(8,128)(2,1)} %bitcast.7, bf16[4,160,640]{2,1,0:T(8,128)(2,1)} %wout_hbm.1), custom_call_target="tpu_custom_call" | custom-call | tf_op jit(solution)/shard_map/pallas_call | solution.py:660
  145.0 0.6 copy.11
  145.6 0.9 copy.12
  146.5 0.9 copy.13
  (1 shorter events, 0.0 us)
Async XLA Ops:
  0.6 0.9 copy-start
